TPU v7x, 32 devices: a whole 2x2x4 slice. The times are simulated.
32 devices in a mesh: seq: 8 (over z, y), blk: 2 (over x), clip: 2 (over core).
Axes of the slice: x: 2, y: 2, z: 4, core: 2. Of those that a mesh axis runs over, the one named last changes fastest.
Arguments:
- modulated: bfloat16 [24576, 3072], P(('clip', 'seq', 'blk')), parts along dimension 0, may hold values from -16 to 16
- mod_gate: float32 [6144], P('clip'), parts along dimension 0, may hold values from 0.5 to 1.5
- w_qkv: bfloat16 [3072, 4608], P(None, 'blk'), may hold values from -0.109375 to 0.109375
- w_out: bfloat16 [1536, 3072], P(None, 'blk'), may hold values from -0.15625 to 0.15625
- kv_tiles: int32 [64, 6], P('clip'), parts along dimension 0, may hold values from 0 to 31, as said below
- kv_count: int32 [64], P('clip'), parts along dimension 0, may hold values from 1 to 6, as said below
Outputs:
- update: bfloat16 [24576, 3072], P(('clip', 'seq', 'blk')), parts along dimension 0
There are 2 independent parts, one for each index of `clip`. A program takes and returns all parts, laid end to end along the dimension named above; an argument that names none is the same for every part. Nothing has to cross between parts.
Inputs may be any that keep to these rules, and one draw needn't show every extreme that they name: Row i of kv_tiles lists 6 different tiles; each of their three tile coordinates differs from tile i's by at most one. `kv_count`: some tile uses all 6 listed tiles.
All inputs are finite; a program needn't handle non-finite values.
Results may differ from a plain program's by a relative error of at most 0.011.
Values may be sent and summed in bfloat16 or wider, within the bound.
No kernel may reach another device: no remote copies, remote signals or barrier semaphores. Data moves between devices by JAX's collectives and lax.ppermute only.
A program may use at most 192 MiB of HBM per device.

v0:
```python
import functools
import math

import jax
import jax.numpy as jnp
from jax import lax
from jax.experimental import pallas as pl
from jax.experimental.pallas import tpu as pltpu
from jax.sharding import PartitionSpec as P

HD = 128
NH = 12
TF = 6
TH = 8
TW = 8
NB = 6
GH = 2
CELLS = TF * TH * TW
AXES = ("seq", "blk", "clip")
HPD = NH // 2
PAIR = 2
BATCHES = ((0, 4), (4, 2))
EXP2_SCALE = math.log2(math.e) / math.sqrt(HD)
MIB = 1 << 20
ROW_BLOCK = 192
AHEAD = 1


def permuted(array, seq_count, target):
    pairs = []
    for seq in range(seq_count):
        for blk in range(2):
            for clip in range(2):
                goal = target(seq // 2, seq % 2, blk, clip)
                if goal is not None:
                    strip, half, blk_to, clip_to = goal
                    pairs.append(
                        ((seq * 2 + blk) * 2 + clip, ((strip * 2 + half) * 2 + blk_to) * 2 + clip_to)
                    )
    return lax.ppermute(array, AXES, pairs)


def after(array, *others):
    return lax.optimization_barrier((array,) + others)[0]


def projection_body(count, spot_out, shared, place, *refs):
    pieces, weight = refs[:count], refs[count]
    query, keyval = refs[count + 1 + shared : count + 3 + shared]
    tokens, columns, blocks, token_sem, weight_sem, out_sem = refs[count + 3 + shared :]
    piece_rows = pieces[0].shape[0]
    loads = []
    for i in range(count):
        start = pl.multiple_of(place[i] * piece_rows, piece_rows)
        loads.append(
            pltpu.make_async_copy(
                pieces[i], tokens.at[pl.ds(start, piece_rows)], token_sem.at[i]
            )
        )
    width = PAIR * 3 * HD
    streams = []
    for batch in range(HPD // PAIR):
        streams.append(
            pltpu.make_async_copy(
                weight.at[:, pl.ds(batch * width, width)], columns.at[batch], weight_sem.at[batch]
            )
        )
    for copy in loads:
        copy.start()
    for copy in streams:
        copy.start()
    for copy in loads:
        copy.wait()
    stores = []
    for batch in range(HPD // PAIR):
        streams[batch].wait()
        total = jnp.dot(tokens[...], columns[batch], preferred_element_type=jnp.float32)
        for spot in range(PAIR):
            head = batch * PAIR + spot
            for kind in range(3):
                start = (spot * 3 + kind) * HD
                blocks[head, kind] = total[:, start : start + HD].astype(jnp.bfloat16)
            for target, some in (
                (query.at[spot_out[0], head], blocks.at[head, 0]),
                (keyval.at[spot_out[1], head], blocks.at[head, pl.ds(1, 2)]),
            ):
                copy = pltpu.make_async_copy(some, target, out_sem.at[len(stores)])
                copy.start()
                stores.append(copy)
    for copy in stores:
        copy.wait()


def project(place, pieces, weight, spot_out, sizes, query, keyval):
    count = len(pieces)
    given = [array for array in (query, keyval) if array is not None]
    aliases = {}
    for array, out in ((query, 0), (keyval, 1)):
        if array is not None:
            aliases[count + 2 + len(aliases)] = out
    piece_rows, depth = pieces[0].shape
    chunk = count * piece_rows
    hbm = pl.BlockSpec(memory_space=pltpu.HBM)
    return pl.pallas_call(
        functools.partial(projection_body, count, spot_out, len(given)),
        out_shape=[
            jax.ShapeDtypeStruct((sizes[0], HPD, chunk, HD), jnp.bfloat16),
            jax.ShapeDtypeStruct((sizes[1], HPD, 2, chunk, HD), jnp.bfloat16),
        ],
        in_specs=[pl.BlockSpec(memory_space=pltpu.SMEM)] + [hbm] * (count + 1 + len(given)),
        out_specs=[hbm] * 2,
        input_output_aliases=aliases,
        scratch_shapes=[
            pltpu.VMEM((chunk, depth), jnp.bfloat16),
            pltpu.VMEM((HPD // PAIR, depth, PAIR * 3 * HD), jnp.bfloat16),
            pltpu.VMEM((HPD, 3, chunk, HD), jnp.bfloat16),
            pltpu.SemaphoreType.DMA((count,)),
            pltpu.SemaphoreType.DMA((HPD // PAIR,)),
            pltpu.SemaphoreType.DMA((2 * HPD,)),
        ],
        compiler_params=pltpu.CompilerParams(vmem_limit_bytes=40 * MIB),
        cost_estimate=pl.CostEstimate(flops=1, bytes_accessed=1, transcendentals=0),
    )(place, *pieces, weight, *given)


def attention_body(first, span, homes, rounds, layers, slots, counts, strips, *refs):
    count = 1 + 3 * (1 + max(group for group, _ in homes))
    queries_in, sources = refs[0], refs[1:count]
    out, query, keyvals, keys, values, query_sems, key_sems = refs[count:]
    chunk = query.shape[1] // rounds
    copies = [[] for _ in range(span)]
    for spot in range(span):
        head = first + spot
        for i in range(rounds):
            for column in range(3):
                at = pl.ds(pl.multiple_of(strips[column * rounds + i] * chunk, chunk), chunk)
                copies[spot].append(
                    pltpu.make_async_copy(
                        sources[3 * homes[i][0] + column].at[homes[i][1], head],
                        keyvals.at[spot, column, :, at],
                        key_sems.at[spot, 3 * i + column],
                    )
                )
            at = pl.ds(pl.multiple_of(strips[i] * chunk, chunk), chunk)
            copies[spot].append(
                pltpu.make_async_copy(
                    queries_in.at[i, head], query.at[spot, at], query_sems.at[spot, i]
                )
            )
    for some in copies:
        for copy in some:
            copy.start()

    def cells(layer, half):
        return [
            pl.ds(pl.multiple_of(((layer * TF + frame) * GH + half) * TH * TW, TH * TW), TH * TW)
            for frame in range(TF)
        ]

    def one_tile(spot, tile, carry):
        layer = tile // GH
        half = tile % GH

        def with_slots(count):
            for slot in range(count):
                found = slots[tile * NB + slot]
                column = found // (layers * GH)
                place = cells(found // GH % layers, found % GH)
                for kind, store in ((0, keys), (1, values)):
                    for frame, rows in enumerate(place):
                        start = slot * CELLS + frame * TH * TW
                        store[start : start + TH * TW] = keyvals[spot, column, kind, rows]
            queries = jnp.concatenate([query[spot, rows] for rows in cells(layer, half)], axis=0)
            results = []
            starts = list(range(0, CELLS, ROW_BLOCK))

            def scores_of(row):
                return lax.dot_general(
                    queries[row : row + ROW_BLOCK],
                    keys[: count * CELLS],
                    (((1,), (1,)), ((), ())),
                    preferred_element_type=jnp.float32,
                )

            ready = [scores_of(row) for row in starts[:AHEAD]]
            for i in range(len(starts)):
                if i + AHEAD < len(starts):
                    ready.append(scores_of(starts[i + AHEAD]))
                scores = ready[i]
                peak = jnp.max(scores, axis=1, keepdims=True)
                weights = jnp.exp2(scores * EXP2_SCALE - peak * EXP2_SCALE)
                denom = jnp.sum(weights, axis=1, keepdims=True)
                mixed = jnp.dot(
                    weights.astype(jnp.bfloat16),
                    values[: count * CELLS],
                    preferred_element_type=jnp.float32,
                )
                results.append(mixed / denom)
            result = jnp.concatenate(results, axis=0).astype(jnp.bfloat16)
            for frame, rows in enumerate(cells(layer, half)):
                out[spot, rows] = result[frame * TH * TW : (frame + 1) * TH * TW]

        for count in range(1, NB + 1):
            pl.when(counts[tile] == count)(functools.partial(with_slots, count))
        return carry

    for spot in range(span):
        for copy in copies[spot]:
            copy.wait()
        lax.fori_loop(0, layers * GH, functools.partial(one_tile, spot), 0)


def attend(first, span, homes, slots, counts, strips, queries_in, sources):
    rounds, _, chunk, _ = queries_in.shape
    tokens = rounds * chunk
    layers = tokens // (TF * GH * TH * TW)
    smem = pl.BlockSpec(memory_space=pltpu.SMEM)
    anywhere = pl.BlockSpec(memory_space=pl.ANY)
    hbm = pl.BlockSpec(memory_space=pltpu.HBM)
    return pl.pallas_call(
        functools.partial(attention_body, first, span, homes, rounds, layers),
        out_shape=jax.ShapeDtypeStruct((span, tokens, HD), jnp.bfloat16),
        in_specs=[smem, smem, smem] + [hbm] + [anywhere] * len(sources),
        out_specs=pl.BlockSpec(memory_space=pltpu.VMEM),
        scratch_shapes=[
            pltpu.VMEM((span, tokens, HD), jnp.bfloat16),
            pltpu.VMEM((span, 3, 2, tokens, HD), jnp.bfloat16),
            pltpu.VMEM((NB * CELLS, HD), jnp.bfloat16),
            pltpu.VMEM((NB * CELLS, HD), jnp.bfloat16),
            pltpu.SemaphoreType.DMA((span, rounds)),
            pltpu.SemaphoreType.DMA((span, 3 * rounds)),
        ],
        compiler_params=pltpu.CompilerParams(vmem_limit_bytes=60 * MIB),
        cost_estimate=pl.CostEstimate(flops=1, bytes_accessed=1, transcendentals=0),
    )(slots, counts, strips, queries_in, *sources)


def output_body(rounds, rows, strips, *refs):
    count = rounds * len(BATCHES) * 2
    pieces = refs[:count]
    w_own, w_got, w_also, gate, out, mixed, weight, sems, weight_sems = refs[count:]
    part = rows * TW
    steps, _, step = weight.shape
    own_half, own_clip = strips[rounds + 1], strips[rounds + 2]
    n = pl.program_id(0)

    @pl.when(n == 0)
    def _():
        copies = []
        for i in range(rounds):
            for batch, (first, span) in enumerate(BATCHES):
                for spot in range(2 * span):
                    column = 2 * first + spot
                    copy = pltpu.make_async_copy(
                        pieces[(i * len(BATCHES) + batch) * 2 + spot // span].at[spot % span],
                        mixed.at[pl.ds(i * 2 * part, 2 * part), pl.ds(column * HD, HD)],
                        sems.at[i, column],
                    )
                    copy.start()
                    copies.append(copy)
        for k in range(steps):
            in_own = (k // (steps // 2)) == own_half
            columns = pl.ds(k % (steps // 2) * step, step)
            for batch, (first, span) in enumerate(BATCHES):
                block = span * HD
                for over_blk in range(2):
                    half = own_half ^ over_blk
                    target = weight.at[k, pl.ds((2 * first + over_blk * span) * HD, block)]
                    sem = weight_sems.at[k, batch * 2 + over_blk]
                    own_row = pl.multiple_of((half * HPD + first) * HD, HD)
                    far_row = first * HD

                    @pl.when(in_own)
                    def _():
                        pltpu.make_async_copy(
                            w_own.at[pl.ds(own_row, block), columns], target, sem
                        ).start()

                    @pl.when(jnp.logical_and(jnp.logical_not(in_own), half == own_clip))
                    def _():
                        pltpu.make_async_copy(
                            w_got.at[pl.ds(far_row, block), columns], target, sem
                        ).start()

                    @pl.when(jnp.logical_and(jnp.logical_not(in_own), half != own_clip))
                    def _():
                        pltpu.make_async_copy(
                            w_also.at[pl.ds(far_row, block), columns], target, sem
                        ).start()

        for copy in copies:
            copy.wait()

    for batch, (first, span) in enumerate(BATCHES):
        for over_blk in range(2):
            pltpu.make_async_copy(
                w_own.at[pl.ds(0, span * HD), pl.ds(0, step)],
                weight.at[n, pl.ds((2 * first + over_blk * span) * HD, span * HD)],
                weight_sems.at[n, batch * 2 + over_blk],
            ).wait()
    product = jnp.dot(mixed[...], weight[n], preferred_element_type=jnp.float32) * gate[...]
    ordered = strips[rounds] == 0
    for i in range(rounds):
        strip = strips[i]
        for row in range(rows):
            base = i * 2 * part + row * TW
            near, far = product[base : base + TW], product[base + part : base + part + TW]
            both = jnp.concatenate(
                [jnp.where(ordered, near, far), jnp.where(ordered, far, near)], axis=0
            )
            out[row, strip] = both.astype(jnp.bfloat16)


def project_out(strips, pieces, weights, gate, rows):
    rounds = len(pieces) // (2 * len(BATCHES))
    depth, width = weights[0].shape[0], gate.shape[1]
    step = 512
    steps = width // step
    anywhere = pl.BlockSpec(memory_space=pl.ANY)
    return pl.pallas_call(
        lambda strips_ref, *refs: output_body(rounds, rows, strips_ref, *refs),
        out_shape=jax.ShapeDtypeStruct((rows, rounds, 2 * TW, width), jnp.bfloat16),
        grid=(steps,),
        in_specs=[pl.BlockSpec(memory_space=pltpu.SMEM)]
        + [anywhere] * (len(pieces) + 3)
        + [pl.BlockSpec((1, step), lambda n: (0, n))],
        out_specs=pl.BlockSpec((rows, rounds, 2 * TW, step), lambda n: (0, 0, 0, n)),
        scratch_shapes=[
            pltpu.VMEM((rounds * rows * 2 * TW, depth), jnp.bfloat16),
            pltpu.VMEM((steps, depth, step), jnp.bfloat16),
            pltpu.SemaphoreType.DMA((rounds, 2 * HPD)),
            pltpu.SemaphoreType.DMA((steps, 2 * len(BATCHES))),
        ],
        compiler_params=pltpu.CompilerParams(vmem_limit_bytes=28 * MIB),
    )(strips, *pieces, *weights, gate)


def local(modulated, mod_gate, w_qkv, w_out, kv_tiles, kv_count):
    tok_rows, depth = modulated.shape
    seq_count = lax.axis_size("seq")
    rounds = seq_count // 2
    rows = tok_rows // (seq_count * TW)
    part = rows * TW
    strip_tokens = rounds * 4 * part
    layers = strip_tokens // (TF * GH * TH * TW)
    seq_index = lax.axis_index("seq")
    strip, half = seq_index // 2, seq_index % 2
    blk, clip = lax.axis_index("blk"), lax.axis_index("clip")

    def swap(array, over_blk, over_clip):
        return permuted(
            array, seq_count, lambda s, h, b, c: (s, h, b ^ over_blk, c ^ over_clip)
        )

    def regroup(array, distance, flip=0):
        return permuted(array, seq_count, lambda s, h, b, c: (s ^ distance, c, b, h ^ flip))

    by_strip = modulated.reshape(rows, rounds, 2, TW, depth)
    order = jnp.stack(
        [
            (clip ^ flip) * 2 + (blk ^ over_blk)
            for flip in range(2)
            for over_blk in range(2)
        ]
    ).astype(jnp.int32)
    units = [(i, flip) for i in range(rounds) for flip in range(2)]
    near = len(units) // 2
    w_half = w_out.shape[0] // 2
    live = {"w": lax.dynamic_slice_in_dim(w_out, clip * w_half, w_half, axis=0)}
    for n, (i, flip) in enumerate(units):
        sent = lax.dynamic_index_in_dim(by_strip, strip ^ i, 1, keepdims=False)
        sent = lax.dynamic_index_in_dim(sent, half ^ flip, 1, keepdims=False)
        live["send", n] = sent.reshape(part, depth)

    def outward(s, h, b, c):
        goal = s + (1 if c else -1)
        return (goal, h, b, 1 - c) if 0 <= goal < rounds else None

    def halo(group):
        live["outer", group] = permuted(live["own", group], seq_count, outward)
        live["inner", group] = swap(live["own", group], 0, 1)

    last_step = near + 1
    when = {}
    for i in range(rounds):
        when[i] = min(2 * i + 2 if i < rounds // 2 else 2 * i - near + 4, last_step)
    members = [
        [i for i in range(rounds) if when[i] < near],
        [i for i in range(rounds) if when[i] == near],
        [i for i in range(rounds) if when[i] == last_step],
    ]
    homes = tuple(
        next((g, some.index(i)) for g, some in enumerate(members) if i in some)
        for i in range(rounds)
    )
    for step in range(last_step + 1):
        before = dict(live)
        fetched = [near + step] if step < near else []
        fetched += [0, 1] if step == 0 else [step + 1] if step + 1 < near else []
        if step == 1:
            mirrored = [0, 1]
        elif 2 <= step < near:
            mirrored = [near + step - 2, step]
        else:
            mirrored = [2 * near - 2, 2 * near - 1] if step == near else []
        for n in fetched:
            live["piece", n] = regroup(live.pop(("send", n)), *units[n])
        for n in mirrored:
            live["mirror", n] = swap(before["piece", n], 1, 0)
        if step == near:
            halo(0)
        if step == last_step:
            halo(1)
            w_got = swap(live.pop("w"), 1, 0)
        for i in range(rounds):
            if when[i] != step:
                continue
            quad = [live.pop((kind, 2 * i + f)) for f in range(2) for kind in ("piece", "mirror")]
            if part % 16:
                quad = [
                    jnp.take(jnp.stack(quad), jnp.argsort(order), axis=0).reshape(4 * part, depth)
                ]
            group, spot = homes[i]
            live["query"], live["own", group] = project(
                order * 0 if part % 16 else order,
                quad,
                w_qkv,
                (i, spot),
                (rounds, len(members[group])),
                live.get("query"),
                live.get(("own", group)),
            )
        if step < last_step:
            names = list(live)
            live = dict(zip(names, lax.optimization_barrier([live[name] for name in names])))
    halo(2)
    query = live["query"]
    sources = [live[kind, group] for group in range(3) for kind in ("own", "outer", "inner")]

    lists = jnp.concatenate([kv_tiles, kv_count[:, None]], axis=1)
    lists = regroup(lists, 0).reshape(layers * GH, seq_count, NB + 1)
    column = strip * 2 + clip
    lists = lax.dynamic_index_in_dim(lists, column, 1, keepdims=False)
    counts = lists[:, NB]
    tiles = lists[:, :NB]
    side = tiles % seq_count - column
    from_outer = (side == 1) == (clip == 1)
    source = jnp.where(side == 0, 0, jnp.where(from_outer, 1, 2))
    slots = (source * (layers * GH) + tiles // seq_count).reshape(-1)

    outer_strip = strip + 2 * clip - 1
    spots = jnp.stack(
        [strip ^ i for i in range(rounds)]
        + [(outer_strip ^ i) & (rounds - 1) for i in range(rounds)]
        + [strip ^ i for i in range(rounds)]
    ).astype(jnp.int32)


    returned, core = {}, None
    for batch, (first, span) in enumerate(BATCHES):
        asked = after(query, core) if batch else query
        result = attend(first, span, homes, slots, counts, spots, asked, sources)
        result = result.reshape(span, rounds, 2, 2, part, HD)
        kept = lax.dynamic_index_in_dim(result, clip, 2, keepdims=False)
        given = lax.dynamic_index_in_dim(result, 1 - clip, 2, keepdims=False)
        core = swap(given, 0, 1)
        if not batch:
            w_also = swap(after(w_got, core), 0, 1)
        both = jnp.stack([kept, core], axis=3)
        for i in range(rounds):
            for over in range(2):
                sent = lax.dynamic_index_in_dim(both, blk ^ over, 2, keepdims=False)
                sent = lax.dynamic_index_in_dim(sent, strip ^ i, 1, keepdims=False)
                returned[batch, i, over] = permuted(
                    sent.reshape(span, 2 * part, HD),
                    seq_count,
                    lambda s, h, b, c: (s ^ i, c, b ^ over, h),
                )

    strips = jnp.stack([strip ^ i for i in range(rounds)] + [half, blk, clip]).astype(jnp.int32)
    flat = [
        returned[batch, i, over]
        for i in range(rounds)
        for batch in range(len(BATCHES))
        for over in range(2)
    ]
    out = project_out(strips, flat, (w_out, w_got, w_also), mod_gate.reshape(1, -1), rows)
    return out.reshape(tok_rows, -1)


def solution(mesh):
    return jax.shard_map(
        local,
        mesh=mesh,
        in_specs=(
            P(("clip", "seq", "blk"), None),
            P("clip"),
            P(None, "blk"),
            P(None, "blk"),
            P("clip", None),
            P("clip"),
        ),
        out_specs=P(("clip", "seq", "blk"), None),
        check_vma=False,
    )
```

profile of v0, /device:TPU:1, one launch (start us, length us, event | category | flops | bytes accessed | tf_op | source)
XLA Modules:
  0.0 337.1 jit_solution(17143797048815518016)
XLA Ops:
  0.0 4.0 %dynamic-slice_bitcast_fusion = (bf16[96,3072]{1,0:T(8,128)(2,1)}, bf16[96,3072]{1,0:T(8,128)(2,1)S(1)}, bf16[96,3072]{1,0:T(8,128)(2,1)S(1)}, bf16[96,3072]{1,0...) fusion(bf16[12,4,2,8,3072]{4,3,2,1,0:T(8,128)(2,1)} %bitcast.90, ...), kind=kLoop, calls=%fused_computation.34 | loop fusion | bytes 9437208 | tf_op jit(solution)/shard_map/reshape | solution.py:373
  4.0 2.1 collective-permute-start.3
  6.1 2.5 collective-permute-start.2
  8.6 3.3 collective-permute-start.1
  11.8 3.3 constant_dynamic-slice_fusion.4
  15.1 5.9 %collective-permute-done.2.refs_0_ = bf16[96,3072]{1,0:T(8,128)(2,1)S(1)} collective-permute-done((bf16[96,3072]{1,0:T(8,128)(2,1)S(1)}, bf16[96,3072]{1,0:T(8,128)(2,1)S(1)}, u32[]{:S(2)}, u32[]{:S(2)}) %collective-permute-start.2) | collective-permute-done | bytes 589856 | tf_op jit(solution)/shard_map/ppermute | solution.py:40
  21.0 14.8 %collective-permute-done.1.refs_0_ = bf16[96,3072]{1,0:T(8,128)(2,1)S(1)} collective-permute-done((bf16[96,3072]{1,0:T(8,128)(2,1)S(1)}, bf16[96,3072]{1,0:T(8,128)(2,1)S(1)}, u32[]{:S(2)}, u32[]{:S(2)}) %collective-permute-start.1) | collective-permute-done | bytes 589856 | tf_op jit(solution)/shard_map/ppermute | solution.py:40
  35.8 4.7 %collective-permute-start.5 = (bf16[96,3072]{1,0:T(8,128)(2,1)S(1)}, bf16[96,3072]{1,0:T(8,128)(2,1)S(1)}, u32[]{:S(2)}, u32[]{:S(2)}) collective-permute-start(bf16[96,3072]{1,0:T(8,128)(2,1)S(1)} %copy-done.29), channel_id=1, source_target_pairs={{0,8},{1,12},{2,10},{3,14},{4,9},{5,13},{6,11},{7,15},{8,0},{9,4},... | collective-permute-start | bytes 1769480 | tf_op jit(solution)/shard_map/ppermute | solution.py:40
  43.6 20.2 %collective-permute-done.4.refs_2_ = bf16[96,3072]{1,0:T(8,128)(2,1)S(1)} collective-permute-done((bf16[96,3072]{1,0:T(8,128)(2,1)}, bf16[96,3072]{1,0:T(8,128)(2,1)S(1)}, u32[]{:S(2)}, u32[]{:S(2)}) %collective-permute-start.4) | collective-permute-done | bytes 589856 | tf_op jit(solution)/shard_map/ppermute | solution.py:40
  63.9 1.3 collective-permute-done.5.refs_0_
  65.9 2.5 collective-permute-done.7.refs_3_
  76.3 13.0 %shard_map.64 = (bf16[4,6,384,128]{3,2,1,0:T(8,128)(2,1)S(1)}, bf16[1,6,2,384,128]{4,3,2,1,0:T(8,128)(2,1)S(1)}) custom-call(s32[4]{0:T(128)S(1)} %pad_add_fusion.1.place, bf16[96,3072]{1,0:T(8,128)(2,1)S(1)} %copy-done.9, bf16[96,3072]{1,0:T(8,128)(2,1)S(1)} %copy-done.11, bf16[96,3072]{1,0:T(8,128)(2,1)S(1)} %copy-done.7, bf16[96,3072]{1,0:T(8,128)(2,1)S(1)} %copy-done.13, ...), custom_call_target="tpu_custom_call" | custom-call | flops 1 | bytes 1 | tf_op jit(solution)/shard_map/pallas_call | solution.py:104
  89.3 7.4 %collective-permute-done.9.refs_2_ = bf16[96,3072]{1,0:T(8,128)(2,1)} collective-permute-done((bf16[96,3072]{1,0:T(8,128)(2,1)}, bf16[96,3072]{1,0:T(8,128)(2,1)}, u32[]{:S(2)}, u32[]{:S(2)}) %collective-permute-start.9) | collective-permute-done | bytes 589856 | tf_op jit(solution)/shard_map/ppermute | solution.py:40
  96.8 1.3 collective-permute-done.11.refs_1_
  98.1 2.0 collective-permute-start.12
  101.5 12.9 %collective-permute-done.12.refs_2_ = bf16[96,3072]{1,0:T(8,128)(2,1)S(1)} collective-permute-done((bf16[96,3072]{1,0:T(8,128)(2,1)S(1)}, bf16[96,3072]{1,0:T(8,128)(2,1)S(1)}, u32[]{:S(2)}, u32[]{:S(2)}) %collective-permute-start.12) | collective-permute-done | bytes 589856 | tf_op jit(solution)/shard_map/ppermute | solution.py:40
  114.8 12.6 %collective-permute-done.14.refs_3_ = bf16[96,3072]{1,0:T(8,128)(2,1)S(1)} collective-permute-done((bf16[96,3072]{1,0:T(8,128)(2,1)}, bf16[96,3072]{1,0:T(8,128)(2,1)S(1)}, u32[]{:S(2)}, u32[]{:S(2)}) %collective-permute-start.14) | collective-permute-done | bytes 589856 | tf_op jit(solution)/shard_map/ppermute | solution.py:40
  128.4 2.8 collective-permute-start.17
  131.2 1.3 collective-permute-start.15
  132.8 12.2 %shard_map.65 = (bf16[4,6,384,128]{3,2,1,0:T(8,128)(2,1)S(1)}, bf16[2,6,2,384,128]{4,3,2,1,0:T(8,128)(2,1)}) custom-call(s32[4]{0:T(128)S(1)} %pad_add_fusion.1.place, bf16[96,3072]{1,0:T(8,128)(2,1)S(1)} %collective-permute-done.5.refs_0_, bf16[96,3072]{1,0:T(8,128)(2,1)} %collective-permute-done.11.refs_1_, ...), custom_call_target="tpu_custom_call", output_to_operand_aliasing={{0}: (6, {})} | custom-call | flops 1 | bytes 1 | tf_op jit(solution)/shard_map/pallas_call | solution.py:104
  145.0 12.1 %shard_map.66 = (bf16[4,6,384,128]{3,2,1,0:T(8,128)(2,1)S(1)}, bf16[2,6,2,384,128]{4,3,2,1,0:T(8,128)(2,1)}) custom-call(s32[4]{0:T(128)S(1)} %pad_add_fusion.1.place, bf16[96,3072]{1,0:T(8,128)(2,1)S(1)} %collective-permute-done.1.refs_0_, bf16[96,3072]{1,0:T(8,128)(2,1)} %collective-permute-done.10.refs_1_, ...), custom_call_target="tpu_custom_call", output_to_operand_aliasing={{0}: (6, {}), {1}: (7, {})} | custom-call | flops 1 | bytes 1 | tf_op jit(solution)/shard_map/pallas_call | solution.py:104
  157.7 4.0 %collective-permute-start.19 = (bf16[2,6,2,384,128]{4,3,2,1,0:T(8,128)(2,1)}, bf16[2,6,2,384,128]{4,3,2,1,0:T(8,128)(2,1)}, u32[]{:S(2)}, u32[]{:S(2)}) collective-permute-start(bf16[2,6,2,384,128]{4,3,2,1,0:T(8,128)(2,1)} %get-tuple-element.128.refs_4_), channel_id=1, source_target_pairs={{1,8},{3,10},{5,12},{7,14},{8,1},{9,16},{10,3},{11,18},{12,5},{13,... | collective-permute-start | bytes 7077896 | tf_op jit(solution)/shard_map/ppermute | solution.py:40
  161.7 1.3 collective-permute-start.41
  163.0 2.4 collective-permute-start
  165.4 13.0 %shard_map.67 = (bf16[4,6,384,128]{3,2,1,0:T(8,128)(2,1)S(1)}, bf16[1,6,2,384,128]{4,3,2,1,0:T(8,128)(2,1)S(1)}) custom-call(s32[4]{0:T(128)S(1)} %pad_add_fusion.1.place, bf16[96,3072]{1,0:T(8,128)(2,1)S(1)} %copy-done.5, bf16[96,3072]{1,0:T(8,128)(2,1)S(1)} %collective-permute-done.15.refs_1_, ...), custom_call_target="tpu_custom_call", output_to_operand_aliasing={{0}: (6, {})} | custom-call | flops 1 | bytes 1 | tf_op jit(solution)/shard_map/pallas_call | solution.py:104
  178.5 1.5 copy-done
  180.6 3.6 %collective-permute-start.21 = (bf16[1,6,2,384,128]{4,3,2,1,0:T(8,128)(2,1)S(1)}, bf16[1,6,2,384,128]{4,3,2,1,0:T(8,128)(2,1)}, u32[]{:S(2)}, u32[]{:S(2)}) collective-permute-start(bf16[1,6,2,384,128]{4,3,2,1,0:T(8,128)(2,1)S(1)} %get-tuple-element.129.refs_7_), channel_id=1, source_target_pairs={{1,8},{3,10},{5,12},{7,14},{8,1},{9,16},{10,3},{11,18},{12,5},{13,... | collective-permute-start | bytes 3538952 | tf_op jit(solution)/shard_map/ppermute | solution.py:40
  188.6 12.8 %collective-permute-done.21.refs_8_ = bf16[1,6,2,384,128]{4,3,2,1,0:T(8,128)(2,1)} collective-permute-done((bf16[1,6,2,384,128]{4,3,2,1,0:T(8,128)(2,1)S(1)}, bf16[1,6,2,384,128]{4,3,2,1,0:T(8,128)(2,1)}, u32[]{:S(2)}, u32[]{:S(2)}) %collective-permute-start.21) | collective-permute-done | bytes 1179680 | tf_op jit(solution)/shard_map/ppermute | solution.py:40
  201.4 25.7 %shard_map.68 = bf16[4,1536,128]{2,1,0:T(8,128)(2,1)} custom-call(s32[24]{0:T(128)} %reshape.168.slots, s32[4]{0:T(128)} %slice_reduce_fusion.counts, s32[12]{0:T(128)} %stack.92.strips, bf16[4,6,384,128]{3,2,1,0:T(8,128)(2,1)} %copy-done, bf16[1,6,2,384,128]{4,3,2,1,0:T(8,128)(2,1)} %copy-done.2, bf16[1,6,2,384,128]{4,3,2,1,0:T(8,128)(2,1)} %copy-done.28, ...), custom_call_target="tpu_custom_call" | custom-call | flops 1 | bytes 1 | tf_op jit(solution)/shard_map/pallas_call | solution.py:220
  227.1 2.4 constant_dynamic-slice_fusion.2
  229.6 2.4 collective-permute-done.23
  234.4 2.4 collective-permute-start.30
  236.8 14.2 %shard_map.69 = bf16[2,1536,128]{2,1,0:T(8,128)(2,1)} custom-call(s32[24]{0:T(128)} %reshape.168.slots, s32[4]{0:T(128)} %slice_reduce_fusion.counts, s32[12]{0:T(128)} %stack.92.strips, bf16[4,6,384,128]{3,2,1,0:T(8,128)(2,1)} %copy-done, bf16[1,6,2,384,128]{4,3,2,1,0:T(8,128)(2,1)} %copy-done.2, bf16[1,6,2,384,128]{4,3,2,1,0:T(8,128)(2,1)} %copy-done.28, ...), custom_call_target="tpu_custom_call" | custom-call | flops 1 | bytes 1 | tf_op jit(solution)/shard_map/pallas_call | solution.py:220
  252.3 10.4 %collective-permute-start.37 = (bf16[4,192,128]{2,1,0:T(8,128)(2,1)S(1)}, bf16[4,192,128]{2,1,0:T(8,128)(2,1)S(1)}, u32[]{:S(2)}, u32[]{:S(2)}) collective-permute-start(bf16[4,192,128]{2,1,0:T(8,128)(2,1)S(1)} %bitcast.102), channel_id=1, source_target_pairs={{0,24},{1,28},{2,26},{3,30},{4,25},{5,29},{6,27},{7,31},{8,16},{9,... | collective-permute-start | bytes 589832 | tf_op jit(solution)/shard_map/ppermute | solution.py:40
  262.7 1.2 fusion
  263.9 1.9 collective-permute-start.24
  266.9 1.3 collective-permute-done.37.refs_12_
  268.2 6.1 %collective-permute-start.29 = (bf16[4,192,128]{2,1,0:T(8,128)(2,1)S(1)}, bf16[4,192,128]{2,1,0:T(8,128)(2,1)S(1)}, u32[]{:S(2)}, u32[]{:S(2)}) collective-permute-start(bf16[4,192,128]{2,1,0:T(8,128)(2,1)S(1)} %bitcast.101), channel_id=1, source_target_pairs={{0,8},{1,12},{2,10},{3,14},{4,9},{5,13},{6,11},{7,15},{8,0},{9,4},... | collective-permute-start | bytes 589832 | tf_op jit(solution)/shard_map/ppermute | solution.py:40
  274.3 2.4 collective-permute-start.33
  277.7 6.2 %collective-permute-start.34 = (bf16[4,192,128]{2,1,0:T(8,128)(2,1)S(1)}, bf16[4,192,128]{2,1,0:T(8,128)(2,1)S(1)}, u32[]{:S(2)}, u32[]{:S(2)}) collective-permute-start(bf16[4,192,128]{2,1,0:T(8,128)(2,1)S(1)} %bitcast.98), channel_id=1, source_target_pairs={{0,18},{1,22},{2,16},{3,20},{4,19},{5,23},{6,17},{7,21},{8,26},{9,... | collective-permute-start | bytes 589832 | tf_op jit(solution)/shard_map/ppermute | solution.py:40
  284.7 10.2 %collective-permute-done.33.refs_8_ = bf16[4,192,128]{2,1,0:T(8,128)(2,1)S(1)} collective-permute-done((bf16[4,192,128]{2,1,0:T(8,128)(2,1)S(1)}, bf16[4,192,128]{2,1,0:T(8,128)(2,1)S(1)}, u32[]{:S(2)}, u32[]{:S(2)}) %collective-permute-start.33) | collective-permute-done | bytes 196640 | tf_op jit(solution)/shard_map/ppermute | solution.py:40
  294.9 3.0 collective-permute-start.39
  298.5 1.9 collective-permute-start.27
  301.1 2.5 collective-permute-start.40
  304.9 4.3 %collective-permute-start.35 = (bf16[2,192,128]{2,1,0:T(8,128)(2,1)}, bf16[2,192,128]{2,1,0:T(8,128)(2,1)}, u32[]{:S(2)}, u32[]{:S(2)}) collective-permute-start(bf16[2,192,128]{2,1,0:T(8,128)(2,1)} %bitcast.44), channel_id=1, source_target_pairs={{0,16},{1,20},{2,18},{3,22},{4,17},{5,21},{6,19},{7,23},{8,24},{9,... | collective-permute-start | bytes 294920 | tf_op jit(solution)/shard_map/ppermute | solution.py:40
  312.1 3.9 %collective-permute-done.32.refs_7_ = bf16[2,192,128]{2,1,0:T(8,128)(2,1)} collective-permute-done((bf16[2,192,128]{2,1,0:T(8,128)(2,1)}, bf16[2,192,128]{2,1,0:T(8,128)(2,1)}, u32[]{:S(2)}, u32[]{:S(2)}) %collective-permute-start.32) | collective-permute-done | bytes 98336 | tf_op jit(solution)/shard_map/ppermute | solution.py:40
  317.1 2.3 copy-done.1
  324.8 11.8 %shard_map.70 = bf16[12,4,16,3072]{3,2,1,0:T(8,128)(2,1)} custom-call(s32[7]{0:T(128)S(1)} %stack.87.strips_ref, bf16[4,192,128]{2,1,0:T(8,128)(2,1)S(1)} %collective-permute-done.24.refs_0_, bf16[4,192,128]{2,1,0:T(8,128)(2,1)S(1)} %copy-done.15, bf16[2,192,128]{2,1,0:T(8,128)(2,1)S(1)} %copy-done.23, bf16[2,192,128]{2,1,0:T(8,128)(2,1)} %collective-permute-done.28.refs_3_, ...), custom_call_target="tpu_custom_call" | custom-call | tf_op jit(solution)/shard_map/pallas_call | solution.py:320
  (133 shorter events, 39.0 us)
Async XLA Ops:
  4.0 11.1 %collective-permute-start.3 = (bf16[96,3072]{1,0:T(8,128)(2,1)}, bf16[96,3072]{1,0:T(8,128)(2,1)S(1)}, u32[]{:S(2)}, u32[]{:S(2)}) collective-permute-start(bf16[96,3072]{1,0:T(8,128)(2,1)} %get-tuple-element.133), channel_id=1, source_target_pairs={{0,1},{1,5},{2,3},{3,7},{4,0},{5,4},{6,2},{7,6},{8,9},{9,13},{10,1... | collective-permute-start | bytes 1769480 | tf_op jit(solution)/shard_map/ppermute | solution.py:40
  6.1 15.0 %collective-permute-start.2 = (bf16[96,3072]{1,0:T(8,128)(2,1)S(1)}, bf16[96,3072]{1,0:T(8,128)(2,1)S(1)}, u32[]{:S(2)}, u32[]{:S(2)}) collective-permute-start(bf16[96,3072]{1,0:T(8,128)(2,1)S(1)} %get-tuple-element.134), channel_id=1, source_target_pairs={{0,0},{1,4},{2,2},{3,6},{4,1},{5,5},{6,3},{7,7},{8,8},{9,12},{10,1... | collective-permute-start | bytes 1769480 | tf_op jit(solution)/shard_map/ppermute | solution.py:40
  8.6 27.3 %collective-permute-start.1 = (bf16[96,3072]{1,0:T(8,128)(2,1)S(1)}, bf16[96,3072]{1,0:T(8,128)(2,1)S(1)}, u32[]{:S(2)}, u32[]{:S(2)}) collective-permute-start(bf16[96,3072]{1,0:T(8,128)(2,1)S(1)} %get-tuple-element.135), channel_id=1, source_target_pairs={{0,16},{1,20},{2,18},{3,22},{4,17},{5,21},{6,19},{7,23},{8,24},{9,... | collective-permute-start | bytes 1769480 | tf_op jit(solution)/shard_map/ppermute | solution.py:40
  11.8 24.0 %copy-start.29 = (bf16[96,3072]{1,0:T(8,128)(2,1)S(1)}, bf16[96,3072]{1,0:T(8,128)(2,1)}, u32[]{:S(2)}) copy-start(bf16[96,3072]{1,0:T(8,128)(2,1)} %get-tuple-element.77) | copy-start | bytes 1769476
  35.8 28.0 %collective-permute-start.4 = (bf16[96,3072]{1,0:T(8,128)(2,1)}, bf16[96,3072]{1,0:T(8,128)(2,1)S(1)}, u32[]{:S(2)}, u32[]{:S(2)}) collective-permute-start(bf16[96,3072]{1,0:T(8,128)(2,1)} %get-tuple-element.76), channel_id=1, source_target_pairs={{0,17},{1,21},{2,19},{3,23},{4,16},{5,20},{6,18},{7,22},{8,25},{9,... | collective-permute-start | bytes 1769480 | tf_op jit(solution)/shard_map/ppermute | solution.py:40
  35.8 29.3 %collective-permute-start.5 = (bf16[96,3072]{1,0:T(8,128)(2,1)S(1)}, bf16[96,3072]{1,0:T(8,128)(2,1)S(1)}, u32[]{:S(2)}, u32[]{:S(2)}) collective-permute-start(bf16[96,3072]{1,0:T(8,128)(2,1)S(1)} %copy-done.29), channel_id=1, source_target_pairs={{0,8},{1,12},{2,10},{3,14},{4,9},{5,13},{6,11},{7,15},{8,0},{9,4},... | collective-permute-start | bytes 1769480 | tf_op jit(solution)/shard_map/ppermute | solution.py:40
  40.5 24.6 %collective-permute-start.6 = (bf16[96,3072]{1,0:T(8,128)(2,1)S(1)}, bf16[96,3072]{1,0:T(8,128)(2,1)S(1)}, u32[]{:S(2)}, u32[]{:S(2)}) collective-permute-start(bf16[96,3072]{1,0:T(8,128)(2,1)S(1)} %collective-permute-done.2.refs_0_), channel_id=1, source_target_pairs={{0,2},{1,3},{2,0},{3,1},{4,6},{5,7},{6,4},{7,5},{8,10},{9,11},{10,... | collective-permute-start | bytes 1769480 | tf_op jit(solution)/shard_map/ppermute | solution.py:40
  42.5 25.9 %collective-permute-start.7 = (bf16[96,3072]{1,0:T(8,128)(2,1)S(1)}, bf16[96,3072]{1,0:T(8,128)(2,1)S(1)}, u32[]{:S(2)}, u32[]{:S(2)}) collective-permute-start(bf16[96,3072]{1,0:T(8,128)(2,1)S(1)} %collective-permute-done.3.refs_2_), channel_id=1, source_target_pairs={{0,2},{1,3},{2,0},{3,1},{4,6},{5,7},{6,4},{7,5},{8,10},{9,11},{10,... | collective-permute-start | bytes 1769480 | tf_op jit(solution)/shard_map/ppermute | solution.py:40
  69.3 20.0 %collective-permute-start.8 = (bf16[96,3072]{1,0:T(8,128)(2,1)}, bf16[96,3072]{1,0:T(8,128)(2,1)S(1)}, u32[]{:S(2)}, u32[]{:S(2)}) collective-permute-start(bf16[96,3072]{1,0:T(8,128)(2,1)} %get-tuple-element.83), channel_id=1, source_target_pairs={{0,24},{1,28},{2,26},{3,30},{4,25},{5,29},{6,27},{7,31},{8,16},{9,... | collective-permute-start | bytes 1769480 | tf_op jit(solution)/shard_map/ppermute | solution.py:40
  70.5 26.3 %collective-permute-start.9 = (bf16[96,3072]{1,0:T(8,128)(2,1)}, bf16[96,3072]{1,0:T(8,128)(2,1)}, u32[]{:S(2)}, u32[]{:S(2)}) collective-permute-start(bf16[96,3072]{1,0:T(8,128)(2,1)} %get-tuple-element.84), channel_id=1, source_target_pairs={{0,9},{1,13},{2,11},{3,15},{4,8},{5,12},{6,10},{7,14},{8,1},{9,5},... | collective-permute-start | bytes 1769480 | tf_op jit(solution)/shard_map/ppermute | solution.py:40
  70.5 26.3 %collective-permute-start.10 = (bf16[96,3072]{1,0:T(8,128)(2,1)S(1)}, bf16[96,3072]{1,0:T(8,128)(2,1)}, u32[]{:S(2)}, u32[]{:S(2)}) collective-permute-start(bf16[96,3072]{1,0:T(8,128)(2,1)S(1)} %collective-permute-done.1.refs_0_), channel_id=1, source_target_pairs={{0,2},{1,3},{2,0},{3,1},{4,6},{5,7},{6,4},{7,5},{8,10},{9,11},{10,... | collective-permute-start | bytes 1769480 | tf_op jit(solution)/shard_map/ppermute | solution.py:40
  71.7 26.4 %collective-permute-start.11 = (bf16[96,3072]{1,0:T(8,128)(2,1)S(1)}, bf16[96,3072]{1,0:T(8,128)(2,1)}, u32[]{:S(2)}, u32[]{:S(2)}) collective-permute-start(bf16[96,3072]{1,0:T(8,128)(2,1)S(1)} %collective-permute-done.5.refs_0_), channel_id=1, source_target_pairs={{0,2},{1,3},{2,0},{3,1},{4,6},{5,7},{6,4},{7,5},{8,10},{9,11},{10,... | collective-permute-start | bytes 1769480 | tf_op jit(solution)/shard_map/ppermute | solution.py:40
  89.3 55.7 %copy-start.2 = (bf16[1,6,2,384,128]{4,3,2,1,0:T(8,128)(2,1)}, bf16[1,6,2,384,128]{4,3,2,1,0:T(8,128)(2,1)S(1)}, u32[]{:S(2)}) copy-start(bf16[1,6,2,384,128]{4,3,2,1,0:T(8,128)(2,1)S(1)} %get-tuple-element.125.refs_1_) | copy-start | bytes 3538948
  89.3 55.7 %copy-start.4 = (bf16[96,3072]{1,0:T(8,128)(2,1)}, bf16[96,3072]{1,0:T(8,128)(2,1)S(1)}, u32[]{:S(2)}) copy-start(bf16[96,3072]{1,0:T(8,128)(2,1)S(1)} %collective-permute-done.8.refs_0_) | copy-start | bytes 1769476
  98.1 16.4 %collective-permute-start.12 = (bf16[96,3072]{1,0:T(8,128)(2,1)S(1)}, bf16[96,3072]{1,0:T(8,128)(2,1)S(1)}, u32[]{:S(2)}, u32[]{:S(2)}) collective-permute-start(bf16[96,3072]{1,0:T(8,128)(2,1)S(1)} %get-tuple-element.101), channel_id=1, source_target_pairs={{0,25},{1,29},{2,27},{3,31},{4,24},{5,28},{6,26},{7,30},{8,17},{9,... | collective-permute-start | bytes 1769480 | tf_op jit(solution)/shard_map/ppermute | solution.py:40
  100.1 14.8 %collective-permute-start.13 = (bf16[96,3072]{1,0:T(8,128)(2,1)S(1)}, bf16[96,3072]{1,0:T(8,128)(2,1)S(1)}, u32[]{:S(2)}, u32[]{:S(2)}) collective-permute-start(bf16[96,3072]{1,0:T(8,128)(2,1)S(1)} %collective-permute-done.4.refs_2_), channel_id=1, source_target_pairs={{0,2},{1,3},{2,0},{3,1},{4,6},{5,7},{6,4},{7,5},{8,10},{9,11},{10,... | collective-permute-start | bytes 1769480 | tf_op jit(solution)/shard_map/ppermute | solution.py:40
  101.3 26.2 %collective-permute-start.14 = (bf16[96,3072]{1,0:T(8,128)(2,1)}, bf16[96,3072]{1,0:T(8,128)(2,1)S(1)}, u32[]{:S(2)}, u32[]{:S(2)}) collective-permute-start(bf16[96,3072]{1,0:T(8,128)(2,1)} %collective-permute-done.9.refs_2_), channel_id=1, source_target_pairs={{0,2},{1,3},{2,0},{3,1},{4,6},{5,7},{6,4},{7,5},{8,10},{9,11},{10,... | collective-permute-start | bytes 1769480 | tf_op jit(solution)/shard_map/ppermute | solution.py:40
  127.5 30.1 %collective-permute-start.18 = (bf16[1,6,2,384,128]{4,3,2,1,0:T(8,128)(2,1)S(1)}, bf16[1,6,2,384,128]{4,3,2,1,0:T(8,128)(2,1)S(1)}, u32[]{:S(2)}, u32[]{:S(2)}) collective-permute-start(bf16[1,6,2,384,128]{4,3,2,1,0:T(8,128)(2,1)S(1)} %get-tuple-element.125.refs_1_), channel_id=1, source_target_pairs={{0,1},{1,0},{2,3},{3,2},{4,5},{5,4},{6,7},{7,6},{8,9},{9,8},{10,11... | collective-permute-start | bytes 3538952 | tf_op jit(solution)/shard_map/ppermute | solution.py:40
  128.4 29.2 %collective-permute-start.17 = (bf16[1,6,2,384,128]{4,3,2,1,0:T(8,128)(2,1)S(1)}, bf16[1,6,2,384,128]{4,3,2,1,0:T(8,128)(2,1)S(1)}, u32[]{:S(2)}, u32[]{:S(2)}) collective-permute-start(bf16[1,6,2,384,128]{4,3,2,1,0:T(8,128)(2,1)S(1)} %get-tuple-element.125.refs_1_), channel_id=1, source_target_pairs={{1,8},{3,10},{5,12},{7,14},{8,1},{9,16},{10,3},{11,18},{12,5},{13,... | collective-permute-start | bytes 3538952 | tf_op jit(solution)/shard_map/ppermute | solution.py:40
  131.2 25.9 %collective-permute-start.15 = (bf16[96,3072]{1,0:T(8,128)(2,1)S(1)}, bf16[96,3072]{1,0:T(8,128)(2,1)S(1)}, u32[]{:S(2)}, u32[]{:S(2)}) collective-permute-start(bf16[96,3072]{1,0:T(8,128)(2,1)S(1)} %collective-permute-done.8.refs_0_), channel_id=1, source_target_pairs={{0,2},{1,3},{2,0},{3,1},{4,6},{5,7},{6,4},{7,5},{8,10},{9,11},{10,... | collective-permute-start | bytes 1769480 | tf_op jit(solution)/shard_map/ppermute | solution.py:40
  132.5 25.1 %collective-permute-start.16 = (bf16[96,3072]{1,0:T(8,128)(2,1)S(1)}, bf16[96,3072]{1,0:T(8,128)(2,1)S(1)}, u32[]{:S(2)}, u32[]{:S(2)}) collective-permute-start(bf16[96,3072]{1,0:T(8,128)(2,1)S(1)} %collective-permute-done.12.refs_2_), channel_id=1, source_target_pairs={{0,2},{1,3},{2,0},{3,1},{4,6},{5,7},{6,4},{7,5},{8,10},{9,11},{10,... | collective-permute-start | bytes 1769480 | tf_op jit(solution)/shard_map/ppermute | solution.py:40
  157.6 43.7 %collective-permute-start.20 = (bf16[2,6,2,384,128]{4,3,2,1,0:T(8,128)(2,1)}, bf16[2,6,2,384,128]{4,3,2,1,0:T(8,128)(2,1)}, u32[]{:S(2)}, u32[]{:S(2)}) collective-permute-start(bf16[2,6,2,384,128]{4,3,2,1,0:T(8,128)(2,1)} %get-tuple-element.128.refs_4_), channel_id=1, source_target_pairs={{0,1},{1,0},{2,3},{3,2},{4,5},{5,4},{6,7},{7,6},{8,9},{9,8},{10,11... | collective-permute-start | bytes 7077896 | tf_op jit(solution)/shard_map/ppermute | solution.py:40
  157.7 43.6 %collective-permute-start.19 = (bf16[2,6,2,384,128]{4,3,2,1,0:T(8,128)(2,1)}, bf16[2,6,2,384,128]{4,3,2,1,0:T(8,128)(2,1)}, u32[]{:S(2)}, u32[]{:S(2)}) collective-permute-start(bf16[2,6,2,384,128]{4,3,2,1,0:T(8,128)(2,1)} %get-tuple-element.128.refs_4_), channel_id=1, source_target_pairs={{1,8},{3,10},{5,12},{7,14},{8,1},{9,16},{10,3},{11,18},{12,5},{13,... | collective-permute-start | bytes 7077896 | tf_op jit(solution)/shard_map/ppermute | solution.py:40
  161.7 67.9 %collective-permute-start.41 = (bf16[768,1536]{1,0:T(8,128)(2,1)}, bf16[768,1536]{1,0:T(8,128)(2,1)S(1)}, u32[]{:S(2)}, u32[]{:S(2)}) collective-permute-start(bf16[768,1536]{1,0:T(8,128)(2,1)} %constant_dynamic-slice_fusion.4), channel_id=1, source_target_pairs={{0,2},{1,3},{2,0},{3,1},{4,6},{5,7},{6,4},{7,5},{8,10},{9,11},{10,... | collective-permute-start | bytes 7077896 | tf_op jit(solution)/shard_map/ppermute | solution.py:40
  163.0 16.9 %collective-permute-start = (s32[32,7]{0,1:T(8,128)S(1)}, s32[32,7]{0,1:T(8,128)S(1)}, u32[]{:S(2)}, u32[]{:S(2)}) collective-permute-start(s32[32,7]{0,1:T(8,128)S(1)} %pad_add_fusion), channel_id=1, source_target_pairs={{0,0},{1,4},{2,2},{3,6},{4,1},{5,5},{6,3},{7,7},{8,8},{9,12},{10,1... | collective-permute-start | bytes 2696 | tf_op jit(solution)/shard_map/ppermute | solution.py:40
  179.9 21.4 %copy-start.3 = (bf16[1,6,2,384,128]{4,3,2,1,0:T(8,128)(2,1)}, bf16[1,6,2,384,128]{4,3,2,1,0:T(8,128)(2,1)S(1)}, u32[]{:S(2)}) copy-start(bf16[1,6,2,384,128]{4,3,2,1,0:T(8,128)(2,1)S(1)} %get-tuple-element.129.refs_7_) | copy-start | bytes 3538948
  179.9 8.6 %collective-permute-start.22 = (bf16[1,6,2,384,128]{4,3,2,1,0:T(8,128)(2,1)S(1)}, bf16[1,6,2,384,128]{4,3,2,1,0:T(8,128)(2,1)}, u32[]{:S(2)}, u32[]{:S(2)}) collective-permute-start(bf16[1,6,2,384,128]{4,3,2,1,0:T(8,128)(2,1)S(1)} %get-tuple-element.129.refs_7_), channel_id=1, source_target_pairs={{0,1},{1,0},{2,3},{3,2},{4,5},{5,4},{6,7},{7,6},{8,9},{9,8},{10,11... | collective-permute-start | bytes 3538952 | tf_op jit(solution)/shard_map/ppermute | solution.py:40
  180.6 20.8 %collective-permute-start.21 = (bf16[1,6,2,384,128]{4,3,2,1,0:T(8,128)(2,1)S(1)}, bf16[1,6,2,384,128]{4,3,2,1,0:T(8,128)(2,1)}, u32[]{:S(2)}, u32[]{:S(2)}) collective-permute-start(bf16[1,6,2,384,128]{4,3,2,1,0:T(8,128)(2,1)S(1)} %get-tuple-element.129.refs_7_), channel_id=1, source_target_pairs={{1,8},{3,10},{5,12},{7,14},{8,1},{9,16},{10,3},{11,18},{12,5},{13,... | collective-permute-start | bytes 3538952 | tf_op jit(solution)/shard_map/ppermute | solution.py:40
  229.5 2.5 collective-permute-start.23
  232.0 85.0 %collective-permute-start.42 = (bf16[768,1536]{1,0:T(8,128)(2,1)S(1)}, bf16[768,1536]{1,0:T(8,128)(2,1)}, u32[]{:S(2)}, u32[]{:S(2)}) collective-permute-start(bf16[768,1536]{1,0:T(8,128)(2,1)S(1)} %collective-permute-done.41.refs_17_), channel_id=1, source_target_pairs={{0,1},{1,0},{2,3},{3,2},{4,5},{5,4},{6,7},{7,6},{8,9},{9,8},{10,11... | collective-permute-start | bytes 7077896 | tf_op jit(solution)/shard_map/ppermute | solution.py:40
  234.4 31.5 %collective-permute-start.30 = (bf16[4,192,128]{2,1,0:T(8,128)(2,1)S(1)}, bf16[4,192,128]{2,1,0:T(8,128)(2,1)S(1)}, u32[]{:S(2)}, u32[]{:S(2)}) collective-permute-start(bf16[4,192,128]{2,1,0:T(8,128)(2,1)S(1)} %bitcast.103), channel_id=1, source_target_pairs={{0,10},{1,14},{2,8},{3,12},{4,11},{5,15},{6,9},{7,13},{8,2},{9,6},... | collective-permute-start | bytes 589832 | tf_op jit(solution)/shard_map/ppermute | solution.py:40
  252.2 25.5 %collective-permute-start.26 = (bf16[2,4,2,96,128]{4,3,0,2,1:T(8,128)(2,1)S(1)}, bf16[2,4,2,96,128]{4,3,0,2,1:T(8,128)(2,1)S(1)}, u32[]{:S(2)}, u32[]{:S(2)}) collective-permute-start(bf16[2,4,2,96,128]{4,3,0,2,1:T(8,128)(2,1)S(1)} %bitcast.97), channel_id=1, source_target_pairs={{0,1},{1,0},{2,3},{3,2},{4,5},{5,4},{6,7},{7,6},{8,9},{9,8},{10,11... | collective-permute-start | bytes 1179656 | tf_op jit(solution)/shard_map/ppermute | solution.py:40
  252.3 16.0 %collective-permute-start.37 = (bf16[4,192,128]{2,1,0:T(8,128)(2,1)S(1)}, bf16[4,192,128]{2,1,0:T(8,128)(2,1)S(1)}, u32[]{:S(2)}, u32[]{:S(2)}) collective-permute-start(bf16[4,192,128]{2,1,0:T(8,128)(2,1)S(1)} %bitcast.102), channel_id=1, source_target_pairs={{0,24},{1,28},{2,26},{3,30},{4,25},{5,29},{6,27},{7,31},{8,16},{9,... | collective-permute-start | bytes 589832 | tf_op jit(solution)/shard_map/ppermute | solution.py:40
  263.9 10.4 %collective-permute-start.24 = (bf16[4,192,128]{2,1,0:T(8,128)(2,1)S(1)}, bf16[4,192,128]{2,1,0:T(8,128)(2,1)S(1)}, u32[]{:S(2)}, u32[]{:S(2)}) collective-permute-start(bf16[4,192,128]{2,1,0:T(8,128)(2,1)S(1)} %bitcast.105), channel_id=1, source_target_pairs={{0,0},{1,4},{2,2},{3,6},{4,1},{5,5},{6,3},{7,7},{8,8},{9,12},{10,1... | collective-permute-start | bytes 589832 | tf_op jit(solution)/shard_map/ppermute | solution.py:40
  265.9 10.9 %collective-permute-start.38 = (bf16[4,192,128]{2,1,0:T(8,128)(2,1)S(1)}, bf16[4,192,128]{2,1,0:T(8,128)(2,1)S(1)}, u32[]{:S(2)}, u32[]{:S(2)}) collective-permute-start(bf16[4,192,128]{2,1,0:T(8,128)(2,1)S(1)} %bitcast.104), channel_id=1, source_target_pairs={{0,26},{1,30},{2,24},{3,28},{4,27},{5,31},{6,25},{7,29},{8,18},{9,... | collective-permute-start | bytes 589832 | tf_op jit(solution)/shard_map/ppermute | solution.py:40
  266.9 50.1 %copy-start.26 = (f32[3072]{0:T(1024)S(1)}, f32[3072]{0:T(1024)}, u32[]{:S(2)}) copy-start(f32[3072]{0:T(1024)} %param.7) | copy-start | bytes 36868
  268.2 16.4 %collective-permute-start.29 = (bf16[4,192,128]{2,1,0:T(8,128)(2,1)S(1)}, bf16[4,192,128]{2,1,0:T(8,128)(2,1)S(1)}, u32[]{:S(2)}, u32[]{:S(2)}) collective-permute-start(bf16[4,192,128]{2,1,0:T(8,128)(2,1)S(1)} %bitcast.101), channel_id=1, source_target_pairs={{0,8},{1,12},{2,10},{3,14},{4,9},{5,13},{6,11},{7,15},{8,0},{9,4},... | collective-permute-start | bytes 589832 | tf_op jit(solution)/shard_map/ppermute | solution.py:40
  274.3 20.6 %collective-permute-start.33 = (bf16[4,192,128]{2,1,0:T(8,128)(2,1)S(1)}, bf16[4,192,128]{2,1,0:T(8,128)(2,1)S(1)}, u32[]{:S(2)}, u32[]{:S(2)}) collective-permute-start(bf16[4,192,128]{2,1,0:T(8,128)(2,1)S(1)} %bitcast.100), channel_id=1, source_target_pairs={{0,16},{1,20},{2,18},{3,22},{4,17},{5,21},{6,19},{7,23},{8,24},{9,... | collective-permute-start | bytes 589832 | tf_op jit(solution)/shard_map/ppermute | solution.py:40
  276.7 21.1 %collective-permute-start.25 = (bf16[4,192,128]{2,1,0:T(8,128)(2,1)S(1)}, bf16[4,192,128]{2,1,0:T(8,128)(2,1)S(1)}, u32[]{:S(2)}, u32[]{:S(2)}) collective-permute-start(bf16[4,192,128]{2,1,0:T(8,128)(2,1)S(1)} %bitcast.99), channel_id=1, source_target_pairs={{0,2},{1,6},{2,0},{3,4},{4,3},{5,7},{6,1},{7,5},{8,10},{9,14},{10,... | collective-permute-start | bytes 589832 | tf_op jit(solution)/shard_map/ppermute | solution.py:40
  277.7 22.7 %collective-permute-start.34 = (bf16[4,192,128]{2,1,0:T(8,128)(2,1)S(1)}, bf16[4,192,128]{2,1,0:T(8,128)(2,1)S(1)}, u32[]{:S(2)}, u32[]{:S(2)}) collective-permute-start(bf16[4,192,128]{2,1,0:T(8,128)(2,1)S(1)} %bitcast.98), channel_id=1, source_target_pairs={{0,18},{1,22},{2,16},{3,20},{4,19},{5,23},{6,17},{7,21},{8,26},{9,... | collective-permute-start | bytes 589832 | tf_op jit(solution)/shard_map/ppermute | solution.py:40
  284.7 19.0 %collective-permute-start.36 = (bf16[2,192,128]{2,1,0:T(8,128)(2,1)S(1)}, bf16[2,192,128]{2,1,0:T(8,128)(2,1)S(1)}, u32[]{:S(2)}, u32[]{:S(2)}) collective-permute-start(bf16[2,192,128]{2,1,0:T(8,128)(2,1)S(1)} %bitcast.109), channel_id=1, source_target_pairs={{0,18},{1,22},{2,16},{3,20},{4,19},{5,23},{6,17},{7,21},{8,26},{9,... | collective-permute-start | bytes 294920 | tf_op jit(solution)/shard_map/ppermute | solution.py:40
  294.9 9.4 %collective-permute-start.39 = (bf16[2,192,128]{2,1,0:T(8,128)(2,1)S(1)}, bf16[2,192,128]{2,1,0:T(8,128)(2,1)S(1)}, u32[]{:S(2)}, u32[]{:S(2)}) collective-permute-start(bf16[2,192,128]{2,1,0:T(8,128)(2,1)S(1)} %bitcast.108), channel_id=1, source_target_pairs={{0,24},{1,28},{2,26},{3,30},{4,25},{5,29},{6,27},{7,31},{8,16},{9,... | collective-permute-start | bytes 294920 | tf_op jit(solution)/shard_map/ppermute | solution.py:40
  298.5 10.7 %collective-permute-start.27 = (bf16[2,192,128]{2,1,0:T(8,128)(2,1)S(1)}, bf16[2,192,128]{2,1,0:T(8,128)(2,1)S(1)}, u32[]{:S(2)}, u32[]{:S(2)}) collective-permute-start(bf16[2,192,128]{2,1,0:T(8,128)(2,1)S(1)} %bitcast.107), channel_id=1, source_target_pairs={{0,0},{1,4},{2,2},{3,6},{4,1},{5,5},{6,3},{7,7},{8,8},{9,12},{10,1... | collective-permute-start | bytes 294920 | tf_op jit(solution)/shard_map/ppermute | solution.py:40
  301.1 9.0 %collective-permute-start.40 = (bf16[2,192,128]{2,1,0:T(8,128)(2,1)S(1)}, bf16[2,192,128]{2,1,0:T(8,128)(2,1)S(1)}, u32[]{:S(2)}, u32[]{:S(2)}) collective-permute-start(bf16[2,192,128]{2,1,0:T(8,128)(2,1)S(1)} %bitcast.106), channel_id=1, source_target_pairs={{0,26},{1,30},{2,24},{3,28},{4,27},{5,31},{6,25},{7,29},{8,18},{9,... | collective-permute-start | bytes 294920 | tf_op jit(solution)/shard_map/ppermute | solution.py:40
  304.3 7.8 %collective-permute-start.31 = (bf16[2,192,128]{2,1,0:T(8,128)(2,1)}, bf16[2,192,128]{2,1,0:T(8,128)(2,1)}, u32[]{:S(2)}, u32[]{:S(2)}) collective-permute-start(bf16[2,192,128]{2,1,0:T(8,128)(2,1)} %bitcast.40), channel_id=1, source_target_pairs={{0,8},{1,12},{2,10},{3,14},{4,9},{5,13},{6,11},{7,15},{8,0},{9,4},... | collective-permute-start | bytes 294920 | tf_op jit(solution)/shard_map/ppermute | solution.py:40
  304.9 7.2 %collective-permute-start.35 = (bf16[2,192,128]{2,1,0:T(8,128)(2,1)}, bf16[2,192,128]{2,1,0:T(8,128)(2,1)}, u32[]{:S(2)}, u32[]{:S(2)}) collective-permute-start(bf16[2,192,128]{2,1,0:T(8,128)(2,1)} %bitcast.44), channel_id=1, source_target_pairs={{0,16},{1,20},{2,18},{3,22},{4,17},{5,21},{6,19},{7,23},{8,24},{9,... | collective-permute-start | bytes 294920 | tf_op jit(solution)/shard_map/ppermute | solution.py:40
  309.8 6.3 %collective-permute-start.32 = (bf16[2,192,128]{2,1,0:T(8,128)(2,1)}, bf16[2,192,128]{2,1,0:T(8,128)(2,1)}, u32[]{:S(2)}, u32[]{:S(2)}) collective-permute-start(bf16[2,192,128]{2,1,0:T(8,128)(2,1)} %bitcast.41), channel_id=1, source_target_pairs={{0,10},{1,14},{2,8},{3,12},{4,11},{5,15},{6,9},{7,13},{8,2},{9,6},... | collective-permute-start | bytes 294920 | tf_op jit(solution)/shard_map/ppermute | solution.py:40
  310.8 6.3 %collective-permute-start.28 = (bf16[2,192,128]{2,1,0:T(8,128)(2,1)}, bf16[2,192,128]{2,1,0:T(8,128)(2,1)}, u32[]{:S(2)}, u32[]{:S(2)}) collective-permute-start(bf16[2,192,128]{2,1,0:T(8,128)(2,1)} %bitcast.37), channel_id=1, source_target_pairs={{0,2},{1,6},{2,0},{3,4},{4,3},{5,7},{6,1},{7,5},{8,10},{9,14},{10,... | collective-permute-start | bytes 294920 | tf_op jit(solution)/shard_map/ppermute | solution.py:40
  (28 other events, 119.4 us)
where the time goes:
time: 343 us; the launch traced here: 337 us
  waiting for transfers between devices  112 us (33%)
  Pallas kernels  102 us (30%)
  starting transfers between devices  81.5 us (24%)
  local copies, waits for them, and re-layouts  37.9 us (11%)
    ppermute x43, waiting for transfers between devices, permuted(): return lax.ppermute(array, AXES, pairs)  112 us
    ppermute x43, starting transfers between devices, permuted(): return lax.ppermute(array, AXES, pairs)  81.5 us
    pallas_call x4, Pallas kernels, project(): pl.pallas_call(functools.partial(projection_body, count, spot_out, len(gi...  50.4 us
    pallas_call x2, Pallas kernels, attend(): pl.pallas_call(functools.partial(attention_body, first, span, homes, roun...  39.9 us
    unnamed x67, local copies, waits for them, and re-layouts  22.2 us
    pallas_call x1, Pallas kernels, project_out(): pl.pallas_call(lambda strips_ref, *refs: output_body(rounds, rows, strips...  11.8 us
  transfers between devices with their start and end apart: 43, of which 18 were waited for; matrix products, arithmetic and copies ran while one was open for 5% of the time, Pallas kernels for 27%

commit v1 on v0

--- a/solution.py
+++ b/solution.py
@@ -19,7 +19,7 @@
 AXES = ("seq", "blk", "clip")
 HPD = NH // 2
 PAIR = 2
-BATCHES = ((0, 4), (4, 2))
+BATCHES = ((0, 3), (3, 3))
 EXP2_SCALE = math.log2(math.e) / math.sqrt(HD)
 MIB = 1 << 20
 ROW_BLOCK = 192
@@ -118,7 +118,7 @@
             pltpu.SemaphoreType.DMA((HPD // PAIR,)),
             pltpu.SemaphoreType.DMA((2 * HPD,)),
         ],
-        compiler_params=pltpu.CompilerParams(vmem_limit_bytes=40 * MIB),
+        compiler_params=pltpu.CompilerParams(vmem_limit_bytes=60 * MIB),
         cost_estimate=pl.CostEstimate(flops=1, bytes_accessed=1, transcendentals=0),
     )(place, *pieces, weight, *given)
 
@@ -331,7 +331,7 @@
             pltpu.SemaphoreType.DMA((rounds, 2 * HPD)),
             pltpu.SemaphoreType.DMA((steps, 2 * len(BATCHES))),
         ],
-        compiler_params=pltpu.CompilerParams(vmem_limit_bytes=28 * MIB),
+        compiler_params=pltpu.CompilerParams(vmem_limit_bytes=60 * MIB),
     )(strips, *pieces, *weights, gate)
 
 
@@ -381,9 +381,7 @@
         live["inner", group] = swap(live["own", group], 0, 1)
 
     last_step = near + 1
-    when = {}
-    for i in range(rounds):
-        when[i] = min(2 * i + 2 if i < rounds // 2 else 2 * i - near + 4, last_step)
+    when = {i: i + 2 for i in range(rounds)}
     members = [
         [i for i in range(rounds) if when[i] < near],
         [i for i in range(rounds) if when[i] == near],
@@ -396,13 +394,8 @@
     for step in range(last_step + 1):
         before = dict(live)
         fetched = [near + step] if step < near else []
-        fetched += [0, 1] if step == 0 else [step + 1] if step + 1 < near else []
-        if step == 1:
-            mirrored = [0, 1]
-        elif 2 <= step < near:
-            mirrored = [near + step - 2, step]
-        else:
-            mirrored = [2 * near - 2, 2 * near - 1] if step == near else []
+        fetched += [n for n in ((0, 1, 2) if step == 0 else (2 * step + 1, 2 * step + 2)) if n < near]
+        mirrored = [2 * step - 2, 2 * step - 1] if 1 <= step <= near else []
         for n in fetched:
             live["piece", n] = regroup(live.pop(("send", n)), *units[n])
         for n in mirrored:
@@ -433,6 +426,7 @@
         if step < last_step:
             names = list(live)
             live = dict(zip(names, lax.optimization_barrier([live[name] for name in names])))
+    live["own", 2] = after(live["own", 2], live["outer", 1])
     halo(2)
     query = live["query"]
     sources = [live[kind, group] for group in range(3) for kind in ("own", "outer", "inner")]
@@ -463,6 +457,9 @@
         result = result.reshape(span, rounds, 2, 2, part, HD)
         kept = lax.dynamic_index_in_dim(result, clip, 2, keepdims=False)
         given = lax.dynamic_index_in_dim(result, 1 - clip, 2, keepdims=False)
+        if batch:
+            early = [returned[0, i, over] for i in range(rounds // 2, rounds) for over in range(2)]
+            given = after(given, *early)
         core = swap(given, 0, 1)
         if not batch:
             w_also = swap(after(w_got, core), 0, 1)

time: 343 us -> 314 us (0.915)
  local copies, waits for them, and re-layouts: 37.9 us -> 20 us
  waiting for transfers between devices: 112 us -> 99.1 us
  Pallas kernels: 102 us -> 110 us
    unnamed x67 -> x63, local copies, waits for them, and re-layouts: 22.2 us -> 5.77 us
    ppermute x43, waiting for transfers between devices: 112 us -> 99.1 us  [permuted(): return lax.ppermute(array, AXES, pairs)]
    pallas_call x4, Pallas kernels: 50.4 us -> 58 us  [project(): pl.pallas_call(functools.partial(projection_body, count, spot_out, len(gi...]
  transfers between devices with their start and end apart: 43 -> 43, of which waited for: 18 -> 17; matrix products, arithmetic and copies ran while one was open for 5% -> 4% of each run, Pallas kernels for 27% -> 31%
where the time goes in v1:
time: 314 us; the launch traced here: 310 us
  Pallas kernels  110 us (35%)
  waiting for transfers between devices  99.1 us (32%)
  starting transfers between devices  78.1 us (25%)
  local copies, waits for them, and re-layouts  20 us (6%)
    ppermute x43, waiting for transfers between devices, permuted(): return lax.ppermute(array, AXES, pairs)  99.1 us
    ppermute x43, starting transfers between devices, permuted(): return lax.ppermute(array, AXES, pairs)  78.1 us
    pallas_call x4, Pallas kernels, project(): pl.pallas_call(functools.partial(projection_body, count, spot_out, len(gi...  58 us
    pallas_call x2, Pallas kernels, attend(): pl.pallas_call(functools.partial(attention_body, first, span, homes, roun...  36.7 us
    pallas_call x1, Pallas kernels, project_out(): pl.pallas_call(lambda strips_ref, *refs: output_body(rounds, rows, strips...  15.2 us
  transfers between devices with their start and end apart: 43, of which 17 were waited for; matrix products, arithmetic and copies ran while one was open for 4% of the time, Pallas kernels for 31%

profile of v1, /device:TPU:1, one launch (start us, length us, event | category | flops | bytes accessed | tf_op | source)
XLA Modules:
  0.0 310.3 jit_solution(8701611622112726246)
XLA Ops:
  0.0 4.1 %dynamic-slice_bitcast_fusion = (bf16[96,3072]{1,0:T(8,128)(2,1)}, bf16[96,3072]{1,0:T(8,128)(2,1)}, bf16[96,3072]{1,0:T(8,128)(2,1)S(1)}, bf16[96,3072]{1,0:T(8...) fusion(bf16[12,4,2,8,3072]{4,3,2,1,0:T(8,128)(2,1)} %bitcast.90, ...), kind=kLoop, calls=%fused_computation.36 | loop fusion | bytes 9437208 | tf_op jit(solution)/shard_map/reshape | solution.py:373
  4.1 3.6 %collective-permute-start.4 = (bf16[96,3072]{1,0:T(8,128)(2,1)}, bf16[96,3072]{1,0:T(8,128)(2,1)S(1)}, u32[]{:S(2)}, u32[]{:S(2)}) collective-permute-start(bf16[96,3072]{1,0:T(8,128)(2,1)} %get-tuple-element.129), channel_id=1, source_target_pairs={{0,8},{1,12},{2,10},{3,14},{4,9},{5,13},{6,11},{7,15},{8,0},{9,4},... | collective-permute-start | bytes 1769480 | tf_op jit(solution)/shard_map/ppermute | solution.py:40
  7.8 3.0 collective-permute-start.2
  10.8 2.8 collective-permute-start.1
  13.5 3.2 %constant_dynamic-slice_fusion.4 = bf16[768,1536]{1,0:T(8,128)(2,1)} fusion(bf16[1536,1536]{1,0:T(8,128)(2,1)} %refs_16_.1, s32[]{:T(128)S(6)} %select_n.136), kind=kLoop, calls=%fused_computation.64 | loop fusion | bytes 4718596 | tf_op jit(solution)/shard_map/dynamic_slice | solution.py:369
  16.8 16.4 %collective-permute-done.4.refs_0_ = bf16[96,3072]{1,0:T(8,128)(2,1)S(1)} collective-permute-done((bf16[96,3072]{1,0:T(8,128)(2,1)}, bf16[96,3072]{1,0:T(8,128)(2,1)S(1)}, u32[]{:S(2)}, u32[]{:S(2)}) %collective-permute-start.4) | collective-permute-done | bytes 589856 | tf_op jit(solution)/shard_map/ppermute | solution.py:40
  34.3 2.7 collective-permute-done.1.refs_0_
  37.0 5.1 %collective-permute-start.6 = (bf16[96,3072]{1,0:T(8,128)(2,1)}, bf16[96,3072]{1,0:T(8,128)(2,1)}, u32[]{:S(2)}, u32[]{:S(2)}) collective-permute-start(bf16[96,3072]{1,0:T(8,128)(2,1)} %get-tuple-element.75), channel_id=1, source_target_pairs={{0,9},{1,13},{2,11},{3,15},{4,8},{5,12},{6,10},{7,14},{8,1},{9,5},... | collective-permute-start | bytes 1769480 | tf_op jit(solution)/shard_map/ppermute | solution.py:40
  43.6 20.9 %collective-permute-done.5.refs_2_ = bf16[96,3072]{1,0:T(8,128)(2,1)S(1)} collective-permute-done((bf16[96,3072]{1,0:T(8,128)(2,1)}, bf16[96,3072]{1,0:T(8,128)(2,1)S(1)}, u32[]{:S(2)}, u32[]{:S(2)}) %collective-permute-start.5) | collective-permute-done | bytes 589856 | tf_op jit(solution)/shard_map/ppermute | solution.py:40
  67.5 4.4 %collective-permute-start.9 = (bf16[96,3072]{1,0:T(8,128)(2,1)}, bf16[96,3072]{1,0:T(8,128)(2,1)S(1)}, u32[]{:S(2)}, u32[]{:S(2)}) collective-permute-start(bf16[96,3072]{1,0:T(8,128)(2,1)} %get-tuple-element.82), channel_id=1, source_target_pairs={{0,24},{1,28},{2,26},{3,30},{4,25},{5,29},{6,27},{7,31},{8,16},{9,... | collective-permute-start | bytes 1769480 | tf_op jit(solution)/shard_map/ppermute | solution.py:40
  74.0 14.5 %shard_map.64 = (bf16[4,6,384,128]{3,2,1,0:T(8,128)(2,1)}, bf16[2,6,2,384,128]{4,3,2,1,0:T(8,128)(2,1)}) custom-call(s32[4]{0:T(128)} %pad_add_fusion.1.place, bf16[96,3072]{1,0:T(8,128)(2,1)} %copy-done.10, bf16[96,3072]{1,0:T(8,128)(2,1)} %copy-done.12, bf16[96,3072]{1,0:T(8,128)(2,1)} %copy-done.9, bf16[96,3072]{1,0:T(8,128)(2,1)} %copy-done.13, ...), custom_call_target="tpu_custom_call" | custom-call | flops 1 | bytes 1 | tf_op jit(solution)/shard_map/pallas_call | solution.py:104
  88.5 10.8 %collective-permute-done.11.refs_3_ = bf16[96,3072]{1,0:T(8,128)(2,1)} collective-permute-done((bf16[96,3072]{1,0:T(8,128)(2,1)}, bf16[96,3072]{1,0:T(8,128)(2,1)}, u32[]{:S(2)}, u32[]{:S(2)}) %collective-permute-start.11) | collective-permute-done | bytes 589856 | tf_op jit(solution)/shard_map/ppermute | solution.py:40
  99.5 1.2 collective-permute-start.13
  101.0 14.5 %shard_map.65 = (bf16[4,6,384,128]{3,2,1,0:T(8,128)(2,1)}, bf16[2,6,2,384,128]{4,3,2,1,0:T(8,128)(2,1)}) custom-call(s32[4]{0:T(128)} %pad_add_fusion.1.place, bf16[96,3072]{1,0:T(8,128)(2,1)} %copy-done.6, bf16[96,3072]{1,0:T(8,128)(2,1)} %collective-permute-done.10.refs_1_, ...), custom_call_target="tpu_custom_call", output_to_operand_aliasing={{0}: (6, {}), {1}: (7, {})} | custom-call | flops 1 | bytes 1 | tf_op jit(solution)/shard_map/pallas_call | solution.py:104
  115.6 9.8 %collective-permute-done.14.refs_3_ = bf16[96,3072]{1,0:T(8,128)(2,1)S(1)} collective-permute-done((bf16[96,3072]{1,0:T(8,128)(2,1)S(1)}, bf16[96,3072]{1,0:T(8,128)(2,1)S(1)}, u32[]{:S(2)}, u32[]{:S(2)}) %collective-permute-start.14) | collective-permute-done | bytes 589856 | tf_op jit(solution)/shard_map/ppermute | solution.py:40
  126.2 2.6 collective-permute-start.18
  128.8 1.9 collective-permute-start.17
  130.7 1.3 collective-permute-start.15
  132.2 14.5 %shard_map.66 = (bf16[4,6,384,128]{3,2,1,0:T(8,128)(2,1)}, bf16[1,6,2,384,128]{4,3,2,1,0:T(8,128)(2,1)}) custom-call(s32[4]{0:T(128)} %pad_add_fusion.1.place, bf16[96,3072]{1,0:T(8,128)(2,1)} %copy-done.5, bf16[96,3072]{1,0:T(8,128)(2,1)} %copy-done.14, bf16[96,3072]{1,0:T(8,128)(2,1)} %copy-done.8, ...), custom_call_target="tpu_custom_call", output_to_operand_aliasing={{0}: (6, {})} | custom-call | flops 1 | bytes 1 | tf_op jit(solution)/shard_map/pallas_call | solution.py:104
  146.8 11.8 %collective-permute-done.16.refs_3_ = bf16[96,3072]{1,0:T(8,128)(2,1)} collective-permute-done((bf16[96,3072]{1,0:T(8,128)(2,1)S(1)}, bf16[96,3072]{1,0:T(8,128)(2,1)}, u32[]{:S(2)}, u32[]{:S(2)}) %collective-permute-start.16) | collective-permute-done | bytes 589856 | tf_op jit(solution)/shard_map/ppermute | solution.py:40
  159.2 3.2 %collective-permute-start.19 = (bf16[1,6,2,384,128]{4,3,2,1,0:T(8,128)(2,1)}, bf16[1,6,2,384,128]{4,3,2,1,0:T(8,128)(2,1)S(1)}, u32[]{:S(2)}, u32[]{:S(2)}) collective-permute-start(bf16[1,6,2,384,128]{4,3,2,1,0:T(8,128)(2,1)} %get-tuple-element.122.refs_4_), channel_id=1, source_target_pairs={{1,8},{3,10},{5,12},{7,14},{8,1},{9,16},{10,3},{11,18},{12,5},{13,... | collective-permute-start | bytes 3538952 | tf_op jit(solution)/shard_map/ppermute | solution.py:40
  162.4 1.3 collective-permute-start.41
  163.7 14.5 %shard_map.67 = (bf16[4,6,384,128]{3,2,1,0:T(8,128)(2,1)}, bf16[1,6,2,384,128]{4,3,2,1,0:T(8,128)(2,1)}) custom-call(s32[4]{0:T(128)} %pad_add_fusion.1.place, bf16[96,3072]{1,0:T(8,128)(2,1)} %copy-done.7, bf16[96,3072]{1,0:T(8,128)(2,1)} %copy-done.15, bf16[96,3072]{1,0:T(8,128)(2,1)} %copy-done.11, ...), custom_call_target="tpu_custom_call", output_to_operand_aliasing={{0}: (6, {})} | custom-call | flops 1 | bytes 1 | tf_op jit(solution)/shard_map/pallas_call | solution.py:104
  178.8 3.0 collective-permute-start.21
  181.8 1.9 collective-permute-start
  184.4 2.8 collective-permute-done
  190.8 6.1 %collective-permute-done.21.refs_8_ = bf16[1,6,2,384,128]{4,3,2,1,0:T(8,128)(2,1)S(1)} collective-permute-done((bf16[1,6,2,384,128]{4,3,2,1,0:T(8,128)(2,1)}, bf16[1,6,2,384,128]{4,3,2,1,0:T(8,128)(2,1)S(1)}, u32[]{:S(2)}, u32[]{:S(2)}) %collective-permute-start.21) | collective-permute-done | bytes 1179680 | tf_op jit(solution)/shard_map/ppermute | solution.py:40
  198.0 18.4 %shard_map.68 = bf16[3,1536,128]{2,1,0:T(8,128)(2,1)} custom-call(s32[24]{0:T(128)} %reshape.168.slots, s32[4]{0:T(128)} %slice_reduce_fusion.counts, s32[12]{0:T(128)} %stack.92.strips, bf16[4,6,384,128]{3,2,1,0:T(8,128)(2,1)} %get-tuple-element.125.refs_0_, bf16[2,6,2,384,128]{4,3,2,1,0:T(8,128)(2,1)} %get-tuple-element.119.refs_1_, ...), custom_call_target="tpu_custom_call" | custom-call | flops 1 | bytes 1 | tf_op jit(solution)/shard_map/pallas_call | solution.py:220
  216.4 1.3 constant_dynamic-slice_fusion.2
  217.8 2.0 collective-permute-done.23
  220.0 3.0 collective-permute-start.29
  224.8 2.9 collective-permute-start.28
  228.9 18.3 %shard_map.69 = bf16[3,1536,128]{2,1,0:T(8,128)(2,1)} custom-call(s32[24]{0:T(128)} %reshape.168.slots, s32[4]{0:T(128)} %slice_reduce_fusion.counts, s32[12]{0:T(128)} %stack.92.strips, bf16[4,6,384,128]{3,2,1,0:T(8,128)(2,1)} %get-tuple-element.125.refs_0_, bf16[2,6,2,384,128]{4,3,2,1,0:T(8,128)(2,1)} %get-tuple-element.119.refs_1_, ...), custom_call_target="tpu_custom_call" | custom-call | flops 1 | bytes 1 | tf_op jit(solution)/shard_map/pallas_call | solution.py:220
  247.3 1.3 constant_dynamic-slice_fusion
  248.7 2.1 collective-permute-start.30
  250.8 8.6 %collective-permute-start.33 = (bf16[3,192,128]{2,1,0:T(8,128)(2,1)S(1)}, bf16[3,192,128]{2,1,0:T(8,128)(2,1)S(1)}, u32[]{:S(2)}, u32[]{:S(2)}) collective-permute-start(bf16[3,192,128]{2,1,0:T(8,128)(2,1)S(1)} %bitcast.101), channel_id=1, source_target_pairs={{0,8},{1,12},{2,10},{3,14},{4,9},{5,13},{6,11},{7,15},{8,0},{9,4},... | collective-permute-start | bytes 442376 | tf_op jit(solution)/shard_map/ppermute | solution.py:40
  259.4 1.9 collective-permute-start.24
  261.5 2.7 collective-permute-start.25
  265.5 2.3 collective-permute-done.24.refs_0_
  267.7 1.9 collective-permute-start.39
  269.6 3.6 %collective-permute-start.31 = (bf16[3,192,128]{2,1,0:T(8,128)(2,1)S(1)}, bf16[3,192,128]{2,1,0:T(8,128)(2,1)S(1)}, u32[]{:S(2)}, u32[]{:S(2)}) collective-permute-start(bf16[3,192,128]{2,1,0:T(8,128)(2,1)S(1)} %bitcast.103), channel_id=1, source_target_pairs={{0,0},{1,4},{2,2},{3,6},{4,1},{5,5},{6,3},{7,7},{8,8},{9,12},{10,1... | collective-permute-start | bytes 442376 | tf_op jit(solution)/shard_map/ppermute | solution.py:40
  274.3 5.5 %collective-permute-done.38.refs_11_ = bf16[3,192,128]{2,1,0:T(8,128)(2,1)S(1)} collective-permute-done((bf16[3,192,128]{2,1,0:T(8,128)(2,1)S(1)}, bf16[3,192,128]{2,1,0:T(8,128)(2,1)S(1)}, u32[]{:S(2)}, u32[]{:S(2)}) %collective-permute-start.38) | collective-permute-done | bytes 147488 | tf_op jit(solution)/shard_map/ppermute | solution.py:40
  279.8 6.0 %collective-permute-start.37 = (bf16[3,192,128]{2,1,0:T(8,128)(2,1)}, bf16[3,192,128]{2,1,0:T(8,128)(2,1)}, u32[]{:S(2)}, u32[]{:S(2)}) collective-permute-start(bf16[3,192,128]{2,1,0:T(8,128)(2,1)} %bitcast.46), channel_id=1, source_target_pairs={{0,16},{1,20},{2,18},{3,22},{4,17},{5,21},{6,19},{7,23},{8,24},{9,... | collective-permute-start | bytes 442376 | tf_op jit(solution)/shard_map/ppermute | solution.py:40
  285.9 2.1 collective-permute-start.32
  288.6 1.6 collective-permute-done.37.refs_10_
  290.2 3.3 %collective-permute-done.36.refs_7_ = bf16[3,192,128]{2,1,0:T(8,128)(2,1)} collective-permute-done((bf16[3,192,128]{2,1,0:T(8,128)(2,1)}, bf16[3,192,128]{2,1,0:T(8,128)(2,1)}, u32[]{:S(2)}, u32[]{:S(2)}) %collective-permute-start.36) | collective-permute-done | bytes 147488 | tf_op jit(solution)/shard_map/ppermute | solution.py:40
  293.6 1.3 copy-done.4
  294.9 15.2 %shard_map.70 = bf16[12,4,16,3072]{3,2,1,0:T(8,128)(2,1)} custom-call(s32[7]{0:T(128)} %stack.87.strips_ref, bf16[3,192,128]{2,1,0:T(8,128)(2,1)} %copy-done.22, bf16[3,192,128]{2,1,0:T(8,128)(2,1)} %copy-done.24, bf16[3,192,128]{2,1,0:T(8,128)(2,1)} %copy-done.27, bf16[3,192,128]{2,1,0:T(8,128)(2,1)} %collective-permute-done.32.refs_3_, ...), custom_call_target="tpu_custom_call" | custom-call | tf_op jit(solution)/shard_map/pallas_call | solution.py:320
  (129 shorter events, 22.3 us)
Async XLA Ops:
  4.1 29.0 %collective-permute-start.4 = (bf16[96,3072]{1,0:T(8,128)(2,1)}, bf16[96,3072]{1,0:T(8,128)(2,1)S(1)}, u32[]{:S(2)}, u32[]{:S(2)}) collective-permute-start(bf16[96,3072]{1,0:T(8,128)(2,1)} %get-tuple-element.129), channel_id=1, source_target_pairs={{0,8},{1,12},{2,10},{3,14},{4,9},{5,13},{6,11},{7,15},{8,0},{9,4},... | collective-permute-start | bytes 1769480 | tf_op jit(solution)/shard_map/ppermute | solution.py:40
  7.8 25.3 %collective-permute-start.3 = (bf16[96,3072]{1,0:T(8,128)(2,1)}, bf16[96,3072]{1,0:T(8,128)(2,1)S(1)}, u32[]{:S(2)}, u32[]{:S(2)}) collective-permute-start(bf16[96,3072]{1,0:T(8,128)(2,1)} %get-tuple-element.130), channel_id=1, source_target_pairs={{0,1},{1,5},{2,3},{3,7},{4,0},{5,4},{6,2},{7,6},{8,9},{9,13},{10,1... | collective-permute-start | bytes 1769480 | tf_op jit(solution)/shard_map/ppermute | solution.py:40
  7.8 26.5 %collective-permute-start.2 = (bf16[96,3072]{1,0:T(8,128)(2,1)S(1)}, bf16[96,3072]{1,0:T(8,128)(2,1)S(1)}, u32[]{:S(2)}, u32[]{:S(2)}) collective-permute-start(bf16[96,3072]{1,0:T(8,128)(2,1)S(1)} %get-tuple-element.131), channel_id=1, source_target_pairs={{0,0},{1,4},{2,2},{3,6},{4,1},{5,5},{6,3},{7,7},{8,8},{9,12},{10,1... | collective-permute-start | bytes 1769480 | tf_op jit(solution)/shard_map/ppermute | solution.py:40
  10.8 26.2 %collective-permute-start.1 = (bf16[96,3072]{1,0:T(8,128)(2,1)S(1)}, bf16[96,3072]{1,0:T(8,128)(2,1)S(1)}, u32[]{:S(2)}, u32[]{:S(2)}) collective-permute-start(bf16[96,3072]{1,0:T(8,128)(2,1)S(1)} %get-tuple-element.132), channel_id=1, source_target_pairs={{0,16},{1,20},{2,18},{3,22},{4,17},{5,21},{6,19},{7,23},{8,24},{9,... | collective-permute-start | bytes 1769480 | tf_op jit(solution)/shard_map/ppermute | solution.py:40
  33.1 55.4 %copy-start.6 = (bf16[96,3072]{1,0:T(8,128)(2,1)}, bf16[96,3072]{1,0:T(8,128)(2,1)S(1)}, u32[]{:S(2)}) copy-start(bf16[96,3072]{1,0:T(8,128)(2,1)S(1)} %collective-permute-done.4.refs_0_) | copy-start | bytes 1769476
  33.1 40.9 %copy-start.9 = (bf16[96,3072]{1,0:T(8,128)(2,1)}, bf16[96,3072]{1,0:T(8,128)(2,1)S(1)}, u32[]{:S(2)}) copy-start(bf16[96,3072]{1,0:T(8,128)(2,1)S(1)} %collective-permute-done.3.refs_2_) | copy-start | bytes 1769476
  34.3 39.7 %copy-start.10 = (bf16[96,3072]{1,0:T(8,128)(2,1)}, bf16[96,3072]{1,0:T(8,128)(2,1)S(1)}, u32[]{:S(2)}) copy-start(bf16[96,3072]{1,0:T(8,128)(2,1)S(1)} %collective-permute-done.2.refs_0_) | copy-start | bytes 1769476
  37.0 62.5 %copy-start.5 = (bf16[96,3072]{1,0:T(8,128)(2,1)}, bf16[96,3072]{1,0:T(8,128)(2,1)S(1)}, u32[]{:S(2)}) copy-start(bf16[96,3072]{1,0:T(8,128)(2,1)S(1)} %collective-permute-done.1.refs_0_) | copy-start | bytes 1769476
  37.0 27.5 %collective-permute-start.5 = (bf16[96,3072]{1,0:T(8,128)(2,1)}, bf16[96,3072]{1,0:T(8,128)(2,1)S(1)}, u32[]{:S(2)}, u32[]{:S(2)}) collective-permute-start(bf16[96,3072]{1,0:T(8,128)(2,1)} %get-tuple-element.74), channel_id=1, source_target_pairs={{0,17},{1,21},{2,19},{3,23},{4,16},{5,20},{6,18},{7,22},{8,25},{9,... | collective-permute-start | bytes 1769480 | tf_op jit(solution)/shard_map/ppermute | solution.py:40
  37.0 27.7 %collective-permute-start.6 = (bf16[96,3072]{1,0:T(8,128)(2,1)}, bf16[96,3072]{1,0:T(8,128)(2,1)}, u32[]{:S(2)}, u32[]{:S(2)}) collective-permute-start(bf16[96,3072]{1,0:T(8,128)(2,1)} %get-tuple-element.75), channel_id=1, source_target_pairs={{0,9},{1,13},{2,11},{3,15},{4,8},{5,12},{6,10},{7,14},{8,1},{9,5},... | collective-permute-start | bytes 1769480 | tf_op jit(solution)/shard_map/ppermute | solution.py:40
  42.1 22.6 %collective-permute-start.7 = (bf16[96,3072]{1,0:T(8,128)(2,1)S(1)}, bf16[96,3072]{1,0:T(8,128)(2,1)S(1)}, u32[]{:S(2)}, u32[]{:S(2)}) collective-permute-start(bf16[96,3072]{1,0:T(8,128)(2,1)S(1)} %collective-permute-done.2.refs_0_), channel_id=1, source_target_pairs={{0,2},{1,3},{2,0},{3,1},{4,6},{5,7},{6,4},{7,5},{8,10},{9,11},{10,... | collective-permute-start | bytes 1769480 | tf_op jit(solution)/shard_map/ppermute | solution.py:40
  43.3 23.3 %collective-permute-start.8 = (bf16[96,3072]{1,0:T(8,128)(2,1)S(1)}, bf16[96,3072]{1,0:T(8,128)(2,1)S(1)}, u32[]{:S(2)}, u32[]{:S(2)}) collective-permute-start(bf16[96,3072]{1,0:T(8,128)(2,1)S(1)} %collective-permute-done.3.refs_2_), channel_id=1, source_target_pairs={{0,2},{1,3},{2,0},{3,1},{4,6},{5,7},{6,4},{7,5},{8,10},{9,11},{10,... | collective-permute-start | bytes 1769480 | tf_op jit(solution)/shard_map/ppermute | solution.py:40
  64.5 36.3 %copy-start.8 = (bf16[96,3072]{1,0:T(8,128)(2,1)}, bf16[96,3072]{1,0:T(8,128)(2,1)S(1)}, u32[]{:S(2)}) copy-start(bf16[96,3072]{1,0:T(8,128)(2,1)S(1)} %collective-permute-done.5.refs_2_) | copy-start | bytes 1769476
  67.5 21.0 %collective-permute-start.9 = (bf16[96,3072]{1,0:T(8,128)(2,1)}, bf16[96,3072]{1,0:T(8,128)(2,1)S(1)}, u32[]{:S(2)}, u32[]{:S(2)}) collective-permute-start(bf16[96,3072]{1,0:T(8,128)(2,1)} %get-tuple-element.82), channel_id=1, source_target_pairs={{0,24},{1,28},{2,26},{3,30},{4,25},{5,29},{6,27},{7,31},{8,16},{9,... | collective-permute-start | bytes 1769480 | tf_op jit(solution)/shard_map/ppermute | solution.py:40
  71.9 16.6 %collective-permute-start.10 = (bf16[96,3072]{1,0:T(8,128)(2,1)S(1)}, bf16[96,3072]{1,0:T(8,128)(2,1)}, u32[]{:S(2)}, u32[]{:S(2)}) collective-permute-start(bf16[96,3072]{1,0:T(8,128)(2,1)S(1)} %collective-permute-done.4.refs_0_), channel_id=1, source_target_pairs={{0,2},{1,3},{2,0},{3,1},{4,6},{5,7},{6,4},{7,5},{8,10},{9,11},{10,... | collective-permute-start | bytes 1769480 | tf_op jit(solution)/shard_map/ppermute | solution.py:40
  73.1 26.2 %collective-permute-start.11 = (bf16[96,3072]{1,0:T(8,128)(2,1)}, bf16[96,3072]{1,0:T(8,128)(2,1)}, u32[]{:S(2)}, u32[]{:S(2)}) collective-permute-start(bf16[96,3072]{1,0:T(8,128)(2,1)} %collective-permute-done.6.refs_2_), channel_id=1, source_target_pairs={{0,2},{1,3},{2,0},{3,1},{4,6},{5,7},{6,4},{7,5},{8,10},{9,11},{10,... | collective-permute-start | bytes 1769480 | tf_op jit(solution)/shard_map/ppermute | solution.py:40
  99.3 16.2 %collective-permute-start.12 = (bf16[96,3072]{1,0:T(8,128)(2,1)}, bf16[96,3072]{1,0:T(8,128)(2,1)S(1)}, u32[]{:S(2)}, u32[]{:S(2)}) collective-permute-start(bf16[96,3072]{1,0:T(8,128)(2,1)} %get-tuple-element.101), channel_id=1, source_target_pairs={{0,25},{1,29},{2,27},{3,31},{4,24},{5,28},{6,26},{7,30},{8,17},{9,... | collective-permute-start | bytes 1769480 | tf_op jit(solution)/shard_map/ppermute | solution.py:40
  99.5 16.1 %collective-permute-start.13 = (bf16[96,3072]{1,0:T(8,128)(2,1)S(1)}, bf16[96,3072]{1,0:T(8,128)(2,1)S(1)}, u32[]{:S(2)}, u32[]{:S(2)}) collective-permute-start(bf16[96,3072]{1,0:T(8,128)(2,1)S(1)} %collective-permute-done.1.refs_0_), channel_id=1, source_target_pairs={{0,2},{1,3},{2,0},{3,1},{4,6},{5,7},{6,4},{7,5},{8,10},{9,11},{10,... | collective-permute-start | bytes 1769480 | tf_op jit(solution)/shard_map/ppermute | solution.py:40
  100.8 24.6 %collective-permute-start.14 = (bf16[96,3072]{1,0:T(8,128)(2,1)S(1)}, bf16[96,3072]{1,0:T(8,128)(2,1)S(1)}, u32[]{:S(2)}, u32[]{:S(2)}) collective-permute-start(bf16[96,3072]{1,0:T(8,128)(2,1)S(1)} %collective-permute-done.5.refs_2_), channel_id=1, source_target_pairs={{0,2},{1,3},{2,0},{3,1},{4,6},{5,7},{6,4},{7,5},{8,10},{9,11},{10,... | collective-permute-start | bytes 1769480 | tf_op jit(solution)/shard_map/ppermute | solution.py:40
  126.2 32.4 %collective-permute-start.18 = (bf16[2,6,2,384,128]{4,3,2,1,0:T(8,128)(2,1)}, bf16[2,6,2,384,128]{4,3,2,1,0:T(8,128)(2,1)S(1)}, u32[]{:S(2)}, u32[]{:S(2)}) collective-permute-start(bf16[2,6,2,384,128]{4,3,2,1,0:T(8,128)(2,1)} %get-tuple-element.119.refs_1_), channel_id=1, source_target_pairs={{0,1},{1,0},{2,3},{3,2},{4,5},{5,4},{6,7},{7,6},{8,9},{9,8},{10,11... | collective-permute-start | bytes 7077896 | tf_op jit(solution)/shard_map/ppermute | solution.py:40
  128.8 30.5 %collective-permute-start.17 = (bf16[2,6,2,384,128]{4,3,2,1,0:T(8,128)(2,1)}, bf16[2,6,2,384,128]{4,3,2,1,0:T(8,128)(2,1)}, u32[]{:S(2)}, u32[]{:S(2)}) collective-permute-start(bf16[2,6,2,384,128]{4,3,2,1,0:T(8,128)(2,1)} %get-tuple-element.119.refs_1_), channel_id=1, source_target_pairs={{1,8},{3,10},{5,12},{7,14},{8,1},{9,16},{10,3},{11,18},{12,5},{13,... | collective-permute-start | bytes 7077896 | tf_op jit(solution)/shard_map/ppermute | solution.py:40
  130.7 16.1 %collective-permute-start.15 = (bf16[96,3072]{1,0:T(8,128)(2,1)}, bf16[96,3072]{1,0:T(8,128)(2,1)S(1)}, u32[]{:S(2)}, u32[]{:S(2)}) collective-permute-start(bf16[96,3072]{1,0:T(8,128)(2,1)} %copy-done.7), channel_id=1, source_target_pairs={{0,2},{1,3},{2,0},{3,1},{4,6},{5,7},{6,4},{7,5},{8,10},{9,11},{10,... | collective-permute-start | bytes 1769480 | tf_op jit(solution)/shard_map/ppermute | solution.py:40
  132.0 26.6 %collective-permute-start.16 = (bf16[96,3072]{1,0:T(8,128)(2,1)S(1)}, bf16[96,3072]{1,0:T(8,128)(2,1)}, u32[]{:S(2)}, u32[]{:S(2)}) collective-permute-start(bf16[96,3072]{1,0:T(8,128)(2,1)S(1)} %collective-permute-done.12.refs_2_), channel_id=1, source_target_pairs={{0,2},{1,3},{2,0},{3,1},{4,6},{5,7},{6,4},{7,5},{8,10},{9,11},{10,... | collective-permute-start | bytes 1769480 | tf_op jit(solution)/shard_map/ppermute | solution.py:40
  159.2 19.0 %collective-permute-start.19 = (bf16[1,6,2,384,128]{4,3,2,1,0:T(8,128)(2,1)}, bf16[1,6,2,384,128]{4,3,2,1,0:T(8,128)(2,1)S(1)}, u32[]{:S(2)}, u32[]{:S(2)}) collective-permute-start(bf16[1,6,2,384,128]{4,3,2,1,0:T(8,128)(2,1)} %get-tuple-element.122.refs_4_), channel_id=1, source_target_pairs={{1,8},{3,10},{5,12},{7,14},{8,1},{9,16},{10,3},{11,18},{12,5},{13,... | collective-permute-start | bytes 3538952 | tf_op jit(solution)/shard_map/ppermute | solution.py:40
  162.4 55.4 %collective-permute-start.41 = (bf16[768,1536]{1,0:T(8,128)(2,1)}, bf16[768,1536]{1,0:T(8,128)(2,1)}, u32[]{:S(2)}, u32[]{:S(2)}) collective-permute-start(bf16[768,1536]{1,0:T(8,128)(2,1)} %constant_dynamic-slice_fusion.4), channel_id=1, source_target_pairs={{0,2},{1,3},{2,0},{3,1},{4,6},{5,7},{6,4},{7,5},{8,10},{9,11},{10,... | collective-permute-start | bytes 7077896 | tf_op jit(solution)/shard_map/ppermute | solution.py:40
  163.7 27.1 %collective-permute-start.20 = (bf16[1,6,2,384,128]{4,3,2,1,0:T(8,128)(2,1)}, bf16[1,6,2,384,128]{4,3,2,1,0:T(8,128)(2,1)}, u32[]{:S(2)}, u32[]{:S(2)}) collective-permute-start(bf16[1,6,2,384,128]{4,3,2,1,0:T(8,128)(2,1)} %get-tuple-element.122.refs_4_), channel_id=1, source_target_pairs={{0,1},{1,0},{2,3},{3,2},{4,5},{5,4},{6,7},{7,6},{8,9},{9,8},{10,11... | collective-permute-start | bytes 3538952 | tf_op jit(solution)/shard_map/ppermute | solution.py:40
  178.2 12.6 %collective-permute-start.22 = (bf16[1,6,2,384,128]{4,3,2,1,0:T(8,128)(2,1)}, bf16[1,6,2,384,128]{4,3,2,1,0:T(8,128)(2,1)S(1)}, u32[]{:S(2)}, u32[]{:S(2)}) collective-permute-start(bf16[1,6,2,384,128]{4,3,2,1,0:T(8,128)(2,1)} %get-tuple-element.124.refs_7_), channel_id=1, source_target_pairs={{0,1},{1,0},{2,3},{3,2},{4,5},{5,4},{6,7},{7,6},{8,9},{9,8},{10,11... | collective-permute-start | bytes 3538952 | tf_op jit(solution)/shard_map/ppermute | solution.py:40
  178.8 18.1 %collective-permute-start.21 = (bf16[1,6,2,384,128]{4,3,2,1,0:T(8,128)(2,1)}, bf16[1,6,2,384,128]{4,3,2,1,0:T(8,128)(2,1)S(1)}, u32[]{:S(2)}, u32[]{:S(2)}) collective-permute-start(bf16[1,6,2,384,128]{4,3,2,1,0:T(8,128)(2,1)} %get-tuple-element.124.refs_7_), channel_id=1, source_target_pairs={{1,8},{3,10},{5,12},{7,14},{8,1},{9,16},{10,3},{11,18},{12,5},{13,... | collective-permute-start | bytes 3538952 | tf_op jit(solution)/shard_map/ppermute | solution.py:40
  181.8 5.3 %collective-permute-start = (s32[32,7]{0,1:T(8,128)S(1)}, s32[32,7]{0,1:T(8,128)}, u32[]{:S(2)}, u32[]{:S(2)}) collective-permute-start(s32[32,7]{0,1:T(8,128)S(1)} %pad_add_fusion), channel_id=1, source_target_pairs={{0,0},{1,4},{2,2},{3,6},{4,1},{5,5},{6,3},{7,7},{8,8},{9,12},{10,1... | collective-permute-start | bytes 2696 | tf_op jit(solution)/shard_map/ppermute | solution.py:40
  217.7 2.1 collective-permute-start.23
  219.8 73.7 %collective-permute-start.42 = (bf16[768,1536]{1,0:T(8,128)(2,1)}, bf16[768,1536]{1,0:T(8,128)(2,1)S(1)}, u32[]{:S(2)}, u32[]{:S(2)}) collective-permute-start(bf16[768,1536]{1,0:T(8,128)(2,1)} %collective-permute-done.41.refs_17_), channel_id=1, source_target_pairs={{0,1},{1,0},{2,3},{3,2},{4,5},{5,4},{6,7},{7,6},{8,9},{9,8},{10,11... | collective-permute-start | bytes 7077896 | tf_op jit(solution)/shard_map/ppermute | solution.py:40
  220.0 28.6 %collective-permute-start.29 = (bf16[3,192,128]{2,1,0:T(8,128)(2,1)S(1)}, bf16[3,192,128]{2,1,0:T(8,128)(2,1)S(1)}, u32[]{:S(2)}, u32[]{:S(2)}) collective-permute-start(bf16[3,192,128]{2,1,0:T(8,128)(2,1)S(1)} %bitcast.106), channel_id=1, source_target_pairs={{0,26},{1,30},{2,24},{3,28},{4,27},{5,31},{6,25},{7,29},{8,18},{9,... | collective-permute-start | bytes 442376 | tf_op jit(solution)/shard_map/ppermute | solution.py:40
  223.8 24.9 %collective-permute-start.26 = (bf16[3,192,128]{2,1,0:T(8,128)(2,1)}, bf16[3,192,128]{2,1,0:T(8,128)(2,1)S(1)}, u32[]{:S(2)}, u32[]{:S(2)}) collective-permute-start(bf16[3,192,128]{2,1,0:T(8,128)(2,1)} %bitcast.35), channel_id=1, source_target_pairs={{0,16},{1,20},{2,18},{3,22},{4,17},{5,21},{6,19},{7,23},{8,24},{9,... | collective-permute-start | bytes 442376 | tf_op jit(solution)/shard_map/ppermute | solution.py:40
  224.8 23.9 %collective-permute-start.28 = (bf16[3,192,128]{2,1,0:T(8,128)(2,1)S(1)}, bf16[3,192,128]{2,1,0:T(8,128)(2,1)S(1)}, u32[]{:S(2)}, u32[]{:S(2)}) collective-permute-start(bf16[3,192,128]{2,1,0:T(8,128)(2,1)S(1)} %bitcast.107), channel_id=1, source_target_pairs={{0,24},{1,28},{2,26},{3,30},{4,25},{5,29},{6,27},{7,31},{8,16},{9,... | collective-permute-start | bytes 442376 | tf_op jit(solution)/shard_map/ppermute | solution.py:40
  227.7 21.0 %collective-permute-start.27 = (bf16[3,192,128]{2,1,0:T(8,128)(2,1)S(1)}, bf16[3,192,128]{2,1,0:T(8,128)(2,1)S(1)}, u32[]{:S(2)}, u32[]{:S(2)}) collective-permute-start(bf16[3,192,128]{2,1,0:T(8,128)(2,1)S(1)} %bitcast.105), channel_id=1, source_target_pairs={{0,18},{1,22},{2,16},{3,20},{4,19},{5,23},{6,17},{7,21},{8,26},{9,... | collective-permute-start | bytes 442376 | tf_op jit(solution)/shard_map/ppermute | solution.py:40
  248.7 12.7 %collective-permute-start.30 = (bf16[3,4,2,96,128]{4,3,0,2,1:T(8,128)(2,1)S(1)}, bf16[3,4,2,96,128]{4,3,0,2,1:T(8,128)(2,1)S(1)}, u32[]{:S(2)}, u32[]{:S(2)}) collective-permute-start(bf16[3,4,2,96,128]{4,3,0,2,1:T(8,128)(2,1)S(1)} %bitcast.97), channel_id=1, source_target_pairs={{0,1},{1,0},{2,3},{3,2},{4,5},{5,4},{6,7},{7,6},{8,9},{9,8},{10,11... | collective-permute-start | bytes 1769480 | tf_op jit(solution)/shard_map/ppermute | solution.py:40
  250.8 14.3 %collective-permute-start.33 = (bf16[3,192,128]{2,1,0:T(8,128)(2,1)S(1)}, bf16[3,192,128]{2,1,0:T(8,128)(2,1)S(1)}, u32[]{:S(2)}, u32[]{:S(2)}) collective-permute-start(bf16[3,192,128]{2,1,0:T(8,128)(2,1)S(1)} %bitcast.101), channel_id=1, source_target_pairs={{0,8},{1,12},{2,10},{3,14},{4,9},{5,13},{6,11},{7,15},{8,0},{9,4},... | collective-permute-start | bytes 442376 | tf_op jit(solution)/shard_map/ppermute | solution.py:40
  259.4 8.3 %collective-permute-start.24 = (bf16[3,192,128]{2,1,0:T(8,128)(2,1)}, bf16[3,192,128]{2,1,0:T(8,128)(2,1)S(1)}, u32[]{:S(2)}, u32[]{:S(2)}) collective-permute-start(bf16[3,192,128]{2,1,0:T(8,128)(2,1)} %bitcast.30), channel_id=1, source_target_pairs={{0,0},{1,4},{2,2},{3,6},{4,1},{5,5},{6,3},{7,7},{8,8},{9,12},{10,1... | collective-permute-start | bytes 442376 | tf_op jit(solution)/shard_map/ppermute | solution.py:40
  261.4 8.3 %collective-permute-start.34 = (bf16[3,192,128]{2,1,0:T(8,128)(2,1)S(1)}, bf16[3,192,128]{2,1,0:T(8,128)(2,1)S(1)}, u32[]{:S(2)}, u32[]{:S(2)}) collective-permute-start(bf16[3,192,128]{2,1,0:T(8,128)(2,1)S(1)} %bitcast.100), channel_id=1, source_target_pairs={{0,10},{1,14},{2,8},{3,12},{4,11},{5,15},{6,9},{7,13},{8,2},{9,6},... | collective-permute-start | bytes 442376 | tf_op jit(solution)/shard_map/ppermute | solution.py:40
  261.5 11.7 %collective-permute-start.25 = (bf16[3,192,128]{2,1,0:T(8,128)(2,1)S(1)}, bf16[3,192,128]{2,1,0:T(8,128)(2,1)S(1)}, u32[]{:S(2)}, u32[]{:S(2)}) collective-permute-start(bf16[3,192,128]{2,1,0:T(8,128)(2,1)S(1)} %bitcast.99), channel_id=1, source_target_pairs={{0,2},{1,6},{2,0},{3,4},{4,3},{5,7},{6,1},{7,5},{8,10},{9,14},{10,... | collective-permute-start | bytes 442376 | tf_op jit(solution)/shard_map/ppermute | solution.py:40
  265.1 14.7 %collective-permute-start.38 = (bf16[3,192,128]{2,1,0:T(8,128)(2,1)S(1)}, bf16[3,192,128]{2,1,0:T(8,128)(2,1)S(1)}, u32[]{:S(2)}, u32[]{:S(2)}) collective-permute-start(bf16[3,192,128]{2,1,0:T(8,128)(2,1)S(1)} %bitcast.108), channel_id=1, source_target_pairs={{0,18},{1,22},{2,16},{3,20},{4,19},{5,23},{6,17},{7,21},{8,26},{9,... | collective-permute-start | bytes 442376 | tf_op jit(solution)/shard_map/ppermute | solution.py:40
  267.7 12.0 %collective-permute-start.39 = (bf16[3,192,128]{2,1,0:T(8,128)(2,1)S(1)}, bf16[3,192,128]{2,1,0:T(8,128)(2,1)S(1)}, u32[]{:S(2)}, u32[]{:S(2)}) collective-permute-start(bf16[3,192,128]{2,1,0:T(8,128)(2,1)S(1)} %bitcast.104), channel_id=1, source_target_pairs={{0,24},{1,28},{2,26},{3,30},{4,25},{5,29},{6,27},{7,31},{8,16},{9,... | collective-permute-start | bytes 442376 | tf_op jit(solution)/shard_map/ppermute | solution.py:40
  269.6 16.2 %collective-permute-start.31 = (bf16[3,192,128]{2,1,0:T(8,128)(2,1)S(1)}, bf16[3,192,128]{2,1,0:T(8,128)(2,1)S(1)}, u32[]{:S(2)}, u32[]{:S(2)}) collective-permute-start(bf16[3,192,128]{2,1,0:T(8,128)(2,1)S(1)} %bitcast.103), channel_id=1, source_target_pairs={{0,0},{1,4},{2,2},{3,6},{4,1},{5,5},{6,3},{7,7},{8,8},{9,12},{10,1... | collective-permute-start | bytes 442376 | tf_op jit(solution)/shard_map/ppermute | solution.py:40
  273.2 12.6 %collective-permute-start.40 = (bf16[3,192,128]{2,1,0:T(8,128)(2,1)S(1)}, bf16[3,192,128]{2,1,0:T(8,128)(2,1)S(1)}, u32[]{:S(2)}, u32[]{:S(2)}) collective-permute-start(bf16[3,192,128]{2,1,0:T(8,128)(2,1)S(1)} %bitcast.102), channel_id=1, source_target_pairs={{0,26},{1,30},{2,24},{3,28},{4,27},{5,31},{6,25},{7,29},{8,18},{9,... | collective-permute-start | bytes 442376 | tf_op jit(solution)/shard_map/ppermute | solution.py:40
  279.8 8.8 %collective-permute-start.35 = (bf16[3,192,128]{2,1,0:T(8,128)(2,1)}, bf16[3,192,128]{2,1,0:T(8,128)(2,1)}, u32[]{:S(2)}, u32[]{:S(2)}) collective-permute-start(bf16[3,192,128]{2,1,0:T(8,128)(2,1)} %bitcast.44), channel_id=1, source_target_pairs={{0,8},{1,12},{2,10},{3,14},{4,9},{5,13},{6,11},{7,15},{8,0},{9,4},... | collective-permute-start | bytes 442376 | tf_op jit(solution)/shard_map/ppermute | solution.py:40
  279.8 10.4 %collective-permute-start.37 = (bf16[3,192,128]{2,1,0:T(8,128)(2,1)}, bf16[3,192,128]{2,1,0:T(8,128)(2,1)}, u32[]{:S(2)}, u32[]{:S(2)}) collective-permute-start(bf16[3,192,128]{2,1,0:T(8,128)(2,1)} %bitcast.46), channel_id=1, source_target_pairs={{0,16},{1,20},{2,18},{3,22},{4,17},{5,21},{6,19},{7,23},{8,24},{9,... | collective-permute-start | bytes 442376 | tf_op jit(solution)/shard_map/ppermute | solution.py:40
  285.8 7.6 %collective-permute-start.36 = (bf16[3,192,128]{2,1,0:T(8,128)(2,1)}, bf16[3,192,128]{2,1,0:T(8,128)(2,1)}, u32[]{:S(2)}, u32[]{:S(2)}) collective-permute-start(bf16[3,192,128]{2,1,0:T(8,128)(2,1)} %bitcast.45), channel_id=1, source_target_pairs={{0,10},{1,14},{2,8},{3,12},{4,11},{5,15},{6,9},{7,13},{8,2},{9,6},... | collective-permute-start | bytes 442376 | tf_op jit(solution)/shard_map/ppermute | solution.py:40
  285.9 7.6 %collective-permute-start.32 = (bf16[3,192,128]{2,1,0:T(8,128)(2,1)}, bf16[3,192,128]{2,1,0:T(8,128)(2,1)}, u32[]{:S(2)}, u32[]{:S(2)}) collective-permute-start(bf16[3,192,128]{2,1,0:T(8,128)(2,1)} %bitcast.41), channel_id=1, source_target_pairs={{0,2},{1,6},{2,0},{3,4},{4,3},{5,7},{6,1},{7,5},{8,10},{9,14},{10,... | collective-permute-start | bytes 442376 | tf_op jit(solution)/shard_map/ppermute | solution.py:40
  (26 other events, 378.4 us)
